TPU v7x, 128 devices: a whole 4x4x4 slice. The times are simulated.
128 devices in a mesh: dom: 64 (over y, x, z), rep: 2 (over core).
Axes of the slice: x: 4, y: 4, z: 4, core: 2. Of those that a mesh axis runs over, the one named last changes fastest.
Arguments:
- features: bfloat16 [131072, 256], P('dom', 'rep'), may hold values from -6 to 6
- cotangent: bfloat16 [131072, 256], P('dom', 'rep'), may hold values from -6 to 6
- self_weight: bfloat16 [256, 256], P('rep'), may hold values from -0.375 to 0.375
- neighbor_weight: bfloat16 [256, 256], P('rep'), may hold values from -0.375 to 0.375
- local_neighbors: int32 [131072, 8], P('dom'), may hold values from 0 to 2047
- hub_rows: int32 [2048], P('dom'), may hold values from 0 to 2047
- hub_neighbors: int32 [131072, 4], P('dom'), may hold values from 0 to 2047
- boundary_rows: int32 [16384], P('dom'), may hold values from 0 to 2047
- send_lists: int32 [64, 64, 128], P('dom'), may hold values from 0 to 255
- received_counts: int32 [64, 64], P('dom'), may hold values from 1 to 128, as said below
- halo_neighbors: int32 [131072, 4], P('dom'), may hold values from 0 to 8064, as said below
Outputs:
- output: bfloat16 [131072, 256], P('dom', 'rep')
- grad_features: bfloat16 [131072, 256], P('dom', 'rep')
- grad_self: float32 [256, 256], P('rep')
- grad_neighbor: float32 [256, 256], P('rep')
Inputs may be any that keep to these rules, and one draw needn't show every extreme that they name: Every row of received_counts has one entry equal to 128 and one entry equal to 1; partition 0 receives 128 live slots from every partition except one. An entry of halo_neighbors for a node of partition d is below the sum of row d of received_counts: it counts the live slots that d receives, ordered by sending partition and then by slot.
All inputs are finite; a program needn't handle non-finite values.
Results may differ from a plain program's by a relative error of at most 0.005.
Values may be sent and summed in bfloat16 or wider, within the bound.
A program may use at most 128 MiB of HBM per device.

v0:
```python
import math

import jax
import jax.numpy as jnp
from jax import lax
from jax.sharding import PartitionSpec as P


def count_table(picked, width, dtype):
    positions = jnp.arange(width, dtype=jnp.int32)[None, :]
    total = jnp.zeros((picked.shape[0], width), dtype)
    for column in range(picked.shape[1]):
        total = total + (picked[:, column : column + 1] == positions).astype(dtype)
    return total


def select_rows(table, picked):
    chooser = count_table(picked[:, None], table.shape[0], table.dtype)
    return jnp.dot(chooser, table, preferred_element_type=jnp.float32).astype(table.dtype)


def add_rows_at(target, picked, values):
    chooser = count_table(picked[:, None], target.shape[0], jnp.float32)
    spread = lax.dot_general(
        chooser,
        values,
        (((0,), (0,)), ((), ())),
        precision=lax.Precision.HIGHEST,
        preferred_element_type=jnp.float32,
    )
    return target + spread


def gather_sum(table, picked, block_rows):
    node_count = picked.shape[0]
    steps_count = node_count // block_rows

    def gather_step(number, total):
        begin = number * block_rows
        piece = lax.dynamic_slice_in_dim(picked, begin, block_rows, 0)
        chooser = count_table(piece, table.shape[0], jnp.bfloat16)
        part_sum = jnp.dot(chooser, table, preferred_element_type=jnp.float32)
        return lax.dynamic_update_slice_in_dim(total, part_sum, begin, 0)

    start_total = jnp.zeros((node_count, table.shape[1]), jnp.float32)
    return lax.fori_loop(0, steps_count, gather_step, start_total)


def scatter_rows(picked, values, width, block_rows):
    steps_count = picked.shape[0] // block_rows

    def scatter_step(number, total):
        begin = number * block_rows
        piece = lax.dynamic_slice_in_dim(picked, begin, block_rows, 0)
        rows_here = lax.dynamic_slice_in_dim(values, begin, block_rows, 0)
        chooser = count_table(piece, width, jnp.float32)
        return total + lax.dot_general(
            chooser,
            rows_here,
            (((0,), (0,)), ((), ())),
            precision=lax.Precision.HIGHEST,
            preferred_element_type=jnp.float32,
        )

    start_total = jnp.zeros((width, values.shape[1]), jnp.float32)
    return lax.fori_loop(0, steps_count, scatter_step, start_total)


def per_device(
    features,
    cotangent,
    self_weight,
    neighbor_weight,
    local_neighbors,
    hub_rows,
    hub_neighbors,
    boundary_rows,
    send_lists,
    received_counts,
    halo_neighbors,
):
    domains = lax.axis_size("dom")
    node_count = features.shape[0]
    half_width = features.shape[1]
    capacity = send_lists.shape[2]
    boundary_count = boundary_rows.shape[0]
    fan_total = local_neighbors.shape[1] + halo_neighbors.shape[1] + hub_neighbors.shape[1]
    counts = received_counts[0]
    block_rows = math.gcd(node_count, 512)
    boundary_feats = select_rows(features, boundary_rows)
    hub_local = select_rows(features, hub_rows)
    hub_table = lax.all_gather(hub_local, "dom", axis=0, tiled=True)
    count_ends = jnp.cumsum(counts)
    passed_ends = count_ends[None, None, :] <= halo_neighbors[:, :, None]
    sender = jnp.minimum(jnp.sum(passed_ends.astype(jnp.int32), -1), domains - 1)
    before = jnp.sum(jnp.where(passed_ends, counts[None, None, :], 0), -1)
    position = jnp.clip(halo_neighbors - before, 0, capacity - 1)
    slot_of = sender * capacity + position
    outgoing = select_rows(boundary_feats, send_lists[0].reshape(-1)).reshape(
        domains, capacity, half_width
    )
    arrived = lax.all_to_all(outgoing, "dom", split_axis=0, concat_axis=0, tiled=True)
    slot_table = arrived.reshape(domains * capacity, half_width)
    summed = gather_sum(features, local_neighbors, block_rows)
    summed = summed + gather_sum(slot_table, slot_of, block_rows)
    summed = summed + gather_sum(hub_table, hub_neighbors, block_rows)
    aggregate = (summed / fan_total).astype(jnp.bfloat16)
    partial_sum = jnp.dot(features, self_weight, preferred_element_type=jnp.float32) + jnp.dot(
        aggregate, neighbor_weight, preferred_element_type=jnp.float32
    )
    pre_act = lax.psum_scatter(partial_sum, "rep", scatter_dimension=1, tiled=True)
    output = jax.nn.silu(pre_act).astype(jnp.bfloat16)
    sigmoid_value = jax.nn.sigmoid(pre_act)
    derivative = sigmoid_value * (1.0 + pre_act * (1.0 - sigmoid_value))
    out_grad = (cotangent.astype(jnp.float32) * derivative).astype(jnp.bfloat16)
    full_grad = lax.all_gather(out_grad, "rep", axis=1, tiled=True)
    over_rows = (((0,), (0,)), ((), ()))
    over_columns = (((1,), (1,)), ((), ()))
    self_term = lax.dot_general(features, full_grad, over_rows, preferred_element_type=jnp.float32)
    neighbor_term = lax.dot_general(
        aggregate, full_grad, over_rows, preferred_element_type=jnp.float32
    )
    self_total, neighbor_total = lax.psum((self_term, neighbor_term), "dom")
    norm_factor = float(node_count * domains) ** (-0.5)
    grad_self = self_total * norm_factor
    grad_neighbor = neighbor_total * norm_factor
    back_agg = (
        lax.dot_general(
            full_grad, neighbor_weight, over_columns, preferred_element_type=jnp.float32
        )
        / fan_total
    )
    gradient = lax.dot_general(
        full_grad, self_weight, over_columns, preferred_element_type=jnp.float32
    )
    gradient = gradient + scatter_rows(local_neighbors, back_agg, node_count, block_rows)
    slot_grads = scatter_rows(slot_of, back_agg, domains * capacity, block_rows)
    hub_grads = scatter_rows(hub_neighbors, back_agg, hub_table.shape[0], block_rows)
    own_hubs = lax.psum_scatter(hub_grads, "dom", scatter_dimension=0, tiled=True)
    gradient = add_rows_at(gradient, hub_rows, own_hubs)
    returned = lax.all_to_all(
        slot_grads.reshape(domains, capacity, half_width).astype(jnp.bfloat16),
        "dom",
        split_axis=0,
        concat_axis=0,
        tiled=True,
    ).astype(jnp.float32)
    boundary_grad = add_rows_at(
        jnp.zeros((boundary_count, half_width), jnp.float32),
        send_lists[0].reshape(-1),
        returned.reshape(domains * capacity, half_width),
    )
    gradient = add_rows_at(gradient, boundary_rows, boundary_grad)
    return (output, gradient.astype(jnp.bfloat16), grad_self, grad_neighbor)


def solution(mesh):
    return jax.shard_map(
        per_device,
        mesh=mesh,
        in_specs=(
            P("dom", "rep"),
            P("dom", "rep"),
            P("rep", None),
            P("rep", None),
            P("dom", None),
            P("dom"),
            P("dom", None),
            P("dom"),
            P("dom", None, None),
            P("dom", None),
            P("dom", None),
        ),
        out_specs=(P("dom", "rep"), P("dom", "rep"), P("rep", None), P("rep", None)),
        check_vma=False,
    )
```

profile of v0, /device:TPU:0, one launch (start us, length us, event | category | flops | bytes accessed | tf_op | source)
XLA Modules:
  0.0 964.7 jit_solution(5582354763107206276)
XLA Ops:
  7.2 4.8 convolution_convert_fusion
  12.0 11.8 %all-to-all-start = ((bf16[64,128,128]{2,1,0:T(8,128)(2,1)}), bf16[64,128,128]{2,1,0:T(8,128)(2,1)}, u32[]{:S(2)}, u32[]{:S(2)}) async-start(bf16[64,128,128]{2,1,0:T(8,128)(2,1)} %bitcast.19), calls=%async_computation | async-start | bytes 4194304 | tf_op jit(solution)/shard_map/all_to_all | solution.py:102
  25.5 22.9 %while.81 = (s32[]{:T(128)}, f32[2048,128]{1,0:T(8,128)}, s32[2048,8]{0,1:T(8,128)S(1)}, bf16[2048,128]{1,0:T(8,128)(2,1)S(1)}, s32[]{:T(128)}, /*index=5*/s32[]...) while((s32[]{:T(128)}, f32[2048,128]{1,0:T(8,128)}, ...), condition=%wide.region_1.2_spmd, body=%wide.region_0.0_spmd.sunk | while | flops 301989888 | bytes 835891 | solution.py:46
  25.6 5.6 fusion.191
  31.3 5.6 fusion.191
  37.1 5.6 fusion.191
  42.8 5.6 fusion.191
  49.4 179.4 %all_gather.6 = bf16[2048,128]{1,0:T(8,128)(2,1)S(1)} all-gather(bf16[32,128]{1,0:T(8,128)(2,1)S(1)} %convolution_convert_fusion.1), channel_id=1, replica_groups=mesh['dom'=64,'rep'=2] {'dom'}, dimensions={0}, use_global_device_ids=true | all-gather | bytes 532480 | tf_op jit(solution)/shard_map/all_gather | solution.py:92
  229.8 13.3 %while.83 = (s32[]{:T(128)}, f32[2048,128]{1,0:T(8,128)}, s32[2048,4]{0,1:T(4,128)S(1)}, bf16[2048,128]{1,0:T(8,128)(2,1)S(1)}, s32[]{:T(128)}, /*index=5*/s32[]...) while((s32[]{:T(128)}, f32[2048,128]{1,0:T(8,128)}, s32[2048,4]{0,1:T(4,128)S(1)}, ...), condition=%wide.region_8.9_spmd, body=%wide.region_7.8_spmd.sunk | while | flops 285212672 | bytes 811219 | solution.py:46
  229.9 3.3 fusion.197
  233.3 3.3 fusion.197
  236.6 3.2 fusion.197
  239.9 3.2 fusion.197
  244.2 44.4 %while.82 = (s32[]{:T(128)}, f32[2048,128]{1,0:T(8,128)}, s32[2048,4]{0,1:T(4,128)S(1)}, bf16[8192,128]{1,0:T(8,128)(2,1)}, s32[]{:T(128)}, /*index=5*/s32[]{:T(...) while((s32[]{:T(128)}, f32[2048,128]{1,0:T(8,128)}, s32[2048,4]{0,1:T(4,128)S(1)}, ...), condition=%wide.region_6.7_spmd, body=%wide.region_5.6_spmd.sunk | while | flops 1140850688 | bytes 2384083 | solution.py:46
  244.3 11.0 %fusion.194 = f32[2048,128]{1,0:T(8,128)} fusion(f32[2048,128]{1,0:T(8,128)} %get-tuple-element.933, s32[]{:T(128)S(6)} %select_n.66, bf16[8192,128]{1,0:T(8,128)(2,1)} %get-tuple-element.946, s32[512]{0:T(512)S(1)} %bitcast.162, s32[512]{0:T(512)S(1)} %bitcast.160, s32[512]{0:T(512)S(1)} %bitcast.161, s32[512]{0:T(512)S(1)} %bitcast.159), kind=kOutput, calls=%fused_computation.50.clone.1 | convolution fusion | flops 1140850688 | bytes 2367492 | tf_op jit(solution)/shard_map/while/body/eval_jaxpr/dot_general | solution.py:42
  255.4 11.0 %fusion.194 = f32[2048,128]{1,0:T(8,128)} fusion(f32[2048,128]{1,0:T(8,128)} %get-tuple-element.933, s32[]{:T(128)S(6)} %select_n.66, bf16[8192,128]{1,0:T(8,128)(2,1)} %get-tuple-element.946, s32[512]{0:T(512)S(1)} %bitcast.162, s32[512]{0:T(512)S(1)} %bitcast.160, s32[512]{0:T(512)S(1)} %bitcast.161, s32[512]{0:T(512)S(1)} %bitcast.159), kind=kOutput, calls=%fused_computation.50.clone.1 | convolution fusion | flops 1140850688 | bytes 2367492 | tf_op jit(solution)/shard_map/while/body/eval_jaxpr/dot_general | solution.py:42
  266.5 11.0 %fusion.194 = f32[2048,128]{1,0:T(8,128)} fusion(f32[2048,128]{1,0:T(8,128)} %get-tuple-element.933, s32[]{:T(128)S(6)} %select_n.66, bf16[8192,128]{1,0:T(8,128)(2,1)} %get-tuple-element.946, s32[512]{0:T(512)S(1)} %bitcast.162, s32[512]{0:T(512)S(1)} %bitcast.160, s32[512]{0:T(512)S(1)} %bitcast.161, s32[512]{0:T(512)S(1)} %bitcast.159), kind=kOutput, calls=%fused_computation.50.clone.1 | convolution fusion | flops 1140850688 | bytes 2367492 | tf_op jit(solution)/shard_map/while/body/eval_jaxpr/dot_general | solution.py:42
  277.6 11.0 %fusion.194 = f32[2048,128]{1,0:T(8,128)} fusion(f32[2048,128]{1,0:T(8,128)} %get-tuple-element.933, s32[]{:T(128)S(6)} %select_n.66, bf16[8192,128]{1,0:T(8,128)(2,1)} %get-tuple-element.946, s32[512]{0:T(512)S(1)} %bitcast.162, s32[512]{0:T(512)S(1)} %bitcast.160, s32[512]{0:T(512)S(1)} %bitcast.161, s32[512]{0:T(512)S(1)} %bitcast.159), kind=kOutput, calls=%fused_computation.50.clone.1 | convolution fusion | flops 1140850688 | bytes 2367492 | tf_op jit(solution)/shard_map/while/body/eval_jaxpr/dot_general | solution.py:42
  288.6 2.0 multiply_convert_fusion.2
  290.6 1.8 convolution_add_fusion
  292.5 5.7 reduce-scatter.3.cloned.1.call-done
  298.1 2.8 multiply_convert_fusion
  301.1 13.2 %all-gather.2.cloned.1.call-done = bf16[2048,256]{1,0:T(8,128)(2,1)} async-done(((bf16[2048,128]{1,0:T(8,128)(2,1)}), bf16[2048,256]{1,0:T(8,128)(2,1)}) %all-gather.2.cloned.1.call-update) | async-done | bytes 1048592 | tf_op jit(solution)/shard_map/all_gather | solution.py:116
  314.3 2.6 convolution_multiply_fusion
  316.9 142.8 %while.86 = (s32[]{:T(128)}, f32[8192,128]{1,0:T(8,128)}, s32[2048,4]{0,1:T(4,128)S(1)}, f32[2048,128]{1,0:T(8,128)}, s32[]{:T(128)}, /*index=5*/s32[]{:T(128)}, s32[]{:T(128)}, s32[]{:T(128)}, s32[]{}, s32[]{}, /*index=10*/s32[]{}) while((s32[]{:T(128)}, f32[8192,128]{1,0:T(8,128)}, s32[2048,4]{0,1:T(4,128)S(1)}, ...), condition=%wide.region_16.17_spmd.clone, body=%wide.region_15.16_spmd.clone.sunk | while | flops 6490685440 | bytes 8675557 | solution.py:66
  317.4 35.0 %fusion.206 = f32[8192,128]{1,0:T(8,128)} fusion(s32[512]{0:T(512)S(1)} %bitcast.150, s32[512]{0:T(512)S(1)} %bitcast.148, s32[512]{0:T(512)S(1)} %bitcast.149, s32[512]{0:T(512)S(1)} %bitcast.147, f32[8192,128]{1,0:T(8,128)} %get-tuple-element.1044, pred[]{:T(512)S(6)} %compare.11, f32[2048,128]{1,0:T(8,128)} %get-tuple-element.1057, s32[]{:T(128)S(6)} %select_n.70), kind=kOutput, calls=%fused_computation.138.clone.1 | convolution fusion | flops 6490685440 | bytes 8658949 | tf_op jit(solution)/shard_map/while/body/eval_jaxpr/dot_general | solution.py:57
  352.5 35.6 %fusion.206 = f32[8192,128]{1,0:T(8,128)} fusion(s32[512]{0:T(512)S(1)} %bitcast.150, s32[512]{0:T(512)S(1)} %bitcast.148, s32[512]{0:T(512)S(1)} %bitcast.149, s32[512]{0:T(512)S(1)} %bitcast.147, f32[8192,128]{1,0:T(8,128)} %get-tuple-element.1044, pred[]{:T(512)S(6)} %compare.11, f32[2048,128]{1,0:T(8,128)} %get-tuple-element.1057, s32[]{:T(128)S(6)} %select_n.70), kind=kOutput, calls=%fused_computation.138.clone.1 | convolution fusion | flops 6490685440 | bytes 8658949 | tf_op jit(solution)/shard_map/while/body/eval_jaxpr/dot_general | solution.py:57
  388.2 35.6 %fusion.206 = f32[8192,128]{1,0:T(8,128)} fusion(s32[512]{0:T(512)S(1)} %bitcast.150, s32[512]{0:T(512)S(1)} %bitcast.148, s32[512]{0:T(512)S(1)} %bitcast.149, s32[512]{0:T(512)S(1)} %bitcast.147, f32[8192,128]{1,0:T(8,128)} %get-tuple-element.1044, pred[]{:T(512)S(6)} %compare.11, f32[2048,128]{1,0:T(8,128)} %get-tuple-element.1057, s32[]{:T(128)S(6)} %select_n.70), kind=kOutput, calls=%fused_computation.138.clone.1 | convolution fusion | flops 6490685440 | bytes 8658949 | tf_op jit(solution)/shard_map/while/body/eval_jaxpr/dot_general | solution.py:57
  423.9 35.6 %fusion.206 = f32[8192,128]{1,0:T(8,128)} fusion(s32[512]{0:T(512)S(1)} %bitcast.150, s32[512]{0:T(512)S(1)} %bitcast.148, s32[512]{0:T(512)S(1)} %bitcast.149, s32[512]{0:T(512)S(1)} %bitcast.147, f32[8192,128]{1,0:T(8,128)} %get-tuple-element.1044, pred[]{:T(512)S(6)} %compare.11, f32[2048,128]{1,0:T(8,128)} %get-tuple-element.1057, s32[]{:T(128)S(6)} %select_n.70), kind=kOutput, calls=%fused_computation.138.clone.1 | convolution fusion | flops 6490685440 | bytes 8658949 | tf_op jit(solution)/shard_map/while/body/eval_jaxpr/dot_general | solution.py:57
  459.7 1.2 fusion.150
  462.1 42.8 %while.85 = (s32[]{:T(128)}, f32[2048,128]{1,0:T(8,128)}, s32[2048,4]{0,1:T(4,128)S(1)}, f32[2048,128]{1,0:T(8,128)}, s32[]{:T(128)}, /*index=5*/s32[]{:T(128)}, s32[]{:T(128)}, s32[]{:T(128)}, s32[]{}, s32[]{}, /*index=10*/s32[]{}) while((s32[]{:T(128)}, f32[2048,128]{1,0:T(8,128)}, s32[2048,4]{0,1:T(4,128)S(1)}, ...), condition=%wide.region_13.14_spmd.clone, body=%wide.region_12.13_spmd.clone.sunk | while | flops 1622671360 | bytes 2384101 | solution.py:66
  462.2 10.3 %fusion.203 = f32[2048,128]{1,0:T(8,128)} fusion(s32[512]{0:T(512)S(1)} %bitcast.154, s32[512]{0:T(512)S(1)} %bitcast.152, s32[512]{0:T(512)S(1)} %bitcast.153, s32[512]{0:T(512)S(1)} %bitcast.151, f32[2048,128]{1,0:T(8,128)} %get-tuple-element.1011, pred[]{:T(512)S(6)} %compare.10, f32[2048,128]{1,0:T(8,128)} %get-tuple-element.1024, s32[]{:T(128)S(6)} %select_n.69), kind=kOutput, calls=%fused_computation.118.clone.1 | convolution fusion | flops 1622671360 | bytes 2367493 | tf_op jit(solution)/shard_map/while/body/eval_jaxpr/dot_general | solution.py:57
  472.6 10.7 %fusion.203 = f32[2048,128]{1,0:T(8,128)} fusion(s32[512]{0:T(512)S(1)} %bitcast.154, s32[512]{0:T(512)S(1)} %bitcast.152, s32[512]{0:T(512)S(1)} %bitcast.153, s32[512]{0:T(512)S(1)} %bitcast.151, f32[2048,128]{1,0:T(8,128)} %get-tuple-element.1011, pred[]{:T(512)S(6)} %compare.10, f32[2048,128]{1,0:T(8,128)} %get-tuple-element.1024, s32[]{:T(128)S(6)} %select_n.69), kind=kOutput, calls=%fused_computation.118.clone.1 | convolution fusion | flops 1622671360 | bytes 2367493 | tf_op jit(solution)/shard_map/while/body/eval_jaxpr/dot_general | solution.py:57
  483.4 10.7 %fusion.203 = f32[2048,128]{1,0:T(8,128)} fusion(s32[512]{0:T(512)S(1)} %bitcast.154, s32[512]{0:T(512)S(1)} %bitcast.152, s32[512]{0:T(512)S(1)} %bitcast.153, s32[512]{0:T(512)S(1)} %bitcast.151, f32[2048,128]{1,0:T(8,128)} %get-tuple-element.1011, pred[]{:T(512)S(6)} %compare.10, f32[2048,128]{1,0:T(8,128)} %get-tuple-element.1024, s32[]{:T(128)S(6)} %select_n.69), kind=kOutput, calls=%fused_computation.118.clone.1 | convolution fusion | flops 1622671360 | bytes 2367493 | tf_op jit(solution)/shard_map/while/body/eval_jaxpr/dot_general | solution.py:57
  494.2 10.7 %fusion.203 = f32[2048,128]{1,0:T(8,128)} fusion(s32[512]{0:T(512)S(1)} %bitcast.154, s32[512]{0:T(512)S(1)} %bitcast.152, s32[512]{0:T(512)S(1)} %bitcast.153, s32[512]{0:T(512)S(1)} %bitcast.151, f32[2048,128]{1,0:T(8,128)} %get-tuple-element.1011, pred[]{:T(512)S(6)} %compare.10, f32[2048,128]{1,0:T(8,128)} %get-tuple-element.1024, s32[]{:T(128)S(6)} %select_n.69), kind=kOutput, calls=%fused_computation.118.clone.1 | convolution fusion | flops 1622671360 | bytes 2367493 | tf_op jit(solution)/shard_map/while/body/eval_jaxpr/dot_general | solution.py:57
  504.9 3.8 convert_element_type.272
  508.7 10.7 %all-to-all-start.1 = ((bf16[64,128,128]{2,1,0:T(8,128)(2,1)}), bf16[64,128,128]{2,1,0:T(8,128)(2,1)}, u32[]{:S(2)}, u32[]{:S(2)}) async-start(bf16[64,128,128]{2,1,0:T(8,128)(2,1)} %bitcast.21), calls=%async_computation.3 | async-start | bytes 4194304 | tf_op jit(solution)/shard_map/all_to_all | solution.py:141
  519.9 47.8 %while.84 = (s32[]{:T(128)}, f32[2048,128]{1,0:T(8,128)S(1)}, s32[2048,8]{0,1:T(8,128)S(1)}, f32[2048,128]{1,0:T(8,128)}, s32[]{:T(128)}, /*index=5*/s32[]{:T(12...) while((s32[]{:T(128)}, f32[2048,128]{1,0:T(8,128)S(1)}, ...), condition=%wide.region_11.12_spmd.clone, body=%wide.region_10.11_spmd.clone.sunk | while | flops 1635254272 | bytes 2408773 | solution.py:66
  520.3 11.7 %fusion.200 = f32[2048,128]{1,0:T(8,128)S(1)} fusion(s32[512]{0:T(512)S(1)} %bitcast.138, s32[512]{0:T(512)S(1)} %bitcast.132, s32[512]{0:T(512)S(1)} %bitcast.133, s32[512]{0:T(512)S(1)} %bitcast.134, s32[512]{0:T(512)S(1)} %bitcast.135, s32[512]{0:T(512)S(1)} %bitcast.136, s32[512]{0:T(512)S(1)} %bitcast.137, s32[512]{0:T(512)S(1)} %bitcast.131, ...), kind=kOutput, calls=%fused_computation.94.clone.1 | convolution fusion | flops 1635254272 | bytes 2375685 | tf_op jit(solution)/shard_map/while/body/eval_jaxpr/dot_general | solution.py:57
  532.1 11.7 %fusion.200 = f32[2048,128]{1,0:T(8,128)S(1)} fusion(s32[512]{0:T(512)S(1)} %bitcast.138, s32[512]{0:T(512)S(1)} %bitcast.132, s32[512]{0:T(512)S(1)} %bitcast.133, s32[512]{0:T(512)S(1)} %bitcast.134, s32[512]{0:T(512)S(1)} %bitcast.135, s32[512]{0:T(512)S(1)} %bitcast.136, s32[512]{0:T(512)S(1)} %bitcast.137, s32[512]{0:T(512)S(1)} %bitcast.131, ...), kind=kOutput, calls=%fused_computation.94.clone.1 | convolution fusion | flops 1635254272 | bytes 2375685 | tf_op jit(solution)/shard_map/while/body/eval_jaxpr/dot_general | solution.py:57
  543.9 11.7 %fusion.200 = f32[2048,128]{1,0:T(8,128)S(1)} fusion(s32[512]{0:T(512)S(1)} %bitcast.138, s32[512]{0:T(512)S(1)} %bitcast.132, s32[512]{0:T(512)S(1)} %bitcast.133, s32[512]{0:T(512)S(1)} %bitcast.134, s32[512]{0:T(512)S(1)} %bitcast.135, s32[512]{0:T(512)S(1)} %bitcast.136, s32[512]{0:T(512)S(1)} %bitcast.137, s32[512]{0:T(512)S(1)} %bitcast.131, ...), kind=kOutput, calls=%fused_computation.94.clone.1 | convolution fusion | flops 1635254272 | bytes 2375685 | tf_op jit(solution)/shard_map/while/body/eval_jaxpr/dot_general | solution.py:57
  555.8 11.7 %fusion.200 = f32[2048,128]{1,0:T(8,128)S(1)} fusion(s32[512]{0:T(512)S(1)} %bitcast.138, s32[512]{0:T(512)S(1)} %bitcast.132, s32[512]{0:T(512)S(1)} %bitcast.133, s32[512]{0:T(512)S(1)} %bitcast.134, s32[512]{0:T(512)S(1)} %bitcast.135, s32[512]{0:T(512)S(1)} %bitcast.136, s32[512]{0:T(512)S(1)} %bitcast.137, s32[512]{0:T(512)S(1)} %bitcast.131, ...), kind=kOutput, calls=%fused_computation.94.clone.1 | convolution fusion | flops 1635254272 | bytes 2375685 | tf_op jit(solution)/shard_map/while/body/eval_jaxpr/dot_general | solution.py:57
  568.7 1.7 convolution_add_fusion.3
  570.4 32.0 %all-reduce.3.cloned.1.call-done = (f32[128,256]{0,1:T(8,128)}, f32[128,256]{0,1:T(8,128)}) async-done(((f32[128,256]{0,1:T(8,128)}, f32[128,256]{0,1:T(8,128)}), (f32[128,256]{0,1:T(8,128)}, f32[128,256]{0,1:T(8,128)})) %all-reduce.3.cloned.1.call-update) | async-done | bytes 262160 | tf_op jit(solution)/shard_map/psum | solution.py:123
  604.9 5.1 fusion.136
  610.0 343.4 %reduce-scatter.5.cloned.1.call-done = f32[32,128]{1,0:T(8,128)} async-done(((f32[2048,128]{1,0:T(8,128)}), f32[32,128]{1,0:T(8,128)}) %reduce-scatter.5.cloned.1.call-update) | async-done | bytes 16400 | tf_op jit(solution)/shard_map/reduce_scatter | solution.py:139
  953.4 1.8 convolution_add_fusion.2
  955.2 2.7 fusion.139
  (79 shorter events, 12.2 us)
Async XLA Ops:
  7.2 283.5 %copy-start = (bf16[128,256]{1,0:T(8,128)(2,1)S(1)}, bf16[128,256]{1,0:T(8,128)(2,1)}, u32[]{:S(2)}) copy-start(bf16[128,256]{1,0:T(8,128)(2,1)} %param.26) | copy-start | bytes 196612
  7.2 16.6 %copy-start.2 = (bf16[2048,128]{1,0:T(8,128)(2,1)S(1)}, bf16[2048,128]{1,0:T(8,128)(2,1)}, u32[]{:S(2)}) copy-start(bf16[2048,128]{1,0:T(8,128)(2,1)} %param.23) | copy-start | bytes 1572868
  7.2 16.6 %copy-start.10 = (s32[32]{0:T(128)S(1)}, s32[32]{0:T(128)}, u32[]{:S(2)}) copy-start(s32[32]{0:T(128)} %param.28) | copy-start | bytes 388
  7.2 16.9 %copy-start.9 = (s32[1,64]{1,0:T(1,128)S(1)}, s32[1,64]{1,0:T(1,128)}, u32[]{:S(2)}) copy-start(s32[1,64]{1,0:T(1,128)} %param.32) | copy-start | bytes 772
  7.2 18.3 %copy-start.4 = (s32[2048,8]{0,1:T(8,128)S(1)}, s32[2048,8]{0,1:T(8,128)}, u32[]{:S(2)}) copy-start(s32[2048,8]{0,1:T(8,128)} %param.27) | copy-start | bytes 196612
  12.0 231.2 %all-to-all-start = ((bf16[64,128,128]{2,1,0:T(8,128)(2,1)}), bf16[64,128,128]{2,1,0:T(8,128)(2,1)}, u32[]{:S(2)}, u32[]{:S(2)}) async-start(bf16[64,128,128]{2,1,0:T(8,128)(2,1)} %bitcast.19), calls=%async_computation | async-start | bytes 4194304 | tf_op jit(solution)/shard_map/all_to_all | solution.py:102
  23.8 274.4 %reduce-scatter.3.cloned.1.call-start = ((), (), s32[]{:S(2)}) async-start(), calls=%async_computation.4 | async-start | bytes 3145728 | tf_op jit(solution)/shard_map/reduce_scatter | solution.py:111
  25.5 22.9 %copy-start.5 = (bf16[128,256]{1,0:T(8,128)(2,1)S(1)}, bf16[128,256]{1,0:T(8,128)(2,1)}, u32[]{:S(2)}) copy-start(bf16[128,256]{1,0:T(8,128)(2,1)} %param.25) | copy-start | bytes 196612
  25.5 23.4 %copy-start.8 = (s32[2048,4]{0,1:T(4,128)S(1)}, s32[2048,4]{0,1:T(4,128)}, u32[]{:S(2)}) copy-start(s32[2048,4]{0,1:T(4,128)} %param.33) | copy-start | bytes 98308
  48.4 181.4 %copy-start.7 = (s32[2048,4]{0,1:T(4,128)S(1)}, s32[2048,4]{0,1:T(4,128)}, u32[]{:S(2)}) copy-start(s32[2048,4]{0,1:T(4,128)} %param.29) | copy-start | bytes 98308
  292.4 21.9 %all-gather.2.cloned.1.call-start = ((), (), s32[]{:S(2)}) async-start(), calls=%async_computation.5 | async-start | bytes 1572864 | tf_op jit(solution)/shard_map/all_gather | solution.py:116
  301.0 301.4 %all-reduce.3.cloned.1.call-start = ((), (), s32[]{:S(2)}) async-start(), calls=%async_computation.7 | async-start | bytes 524288 | tf_op jit(solution)/shard_map/psum | solution.py:123
  316.9 142.8 %copy-start.1 = (bf16[2048,256]{1,0:T(8,128)(2,1)S(1)}, bf16[2048,256]{1,0:T(8,128)(2,1)}, u32[]{:S(2)}) copy-start(bf16[2048,256]{1,0:T(8,128)(2,1)} %all-gather.2.cloned.1.call-done) | copy-start | bytes 3145732
  508.7 96.2 %all-to-all-start.1 = ((bf16[64,128,128]{2,1,0:T(8,128)(2,1)}), bf16[64,128,128]{2,1,0:T(8,128)(2,1)}, u32[]{:S(2)}, u32[]{:S(2)}) async-start(bf16[64,128,128]{2,1,0:T(8,128)(2,1)} %bitcast.21), calls=%async_computation.3 | async-start | bytes 4194304 | tf_op jit(solution)/shard_map/all_to_all | solution.py:141
  519.3 434.0 %reduce-scatter.5.cloned.1.call-start = ((), (), s32[]{:S(2)}) async-start(), calls=%async_computation.6 | async-start | bytes 1064960 | tf_op jit(solution)/shard_map/reduce_scatter | solution.py:139
  519.9 48.8 %copy-start.6 = (bf16[128,256]{1,0:T(8,128)(2,1)S(1)}, bf16[128,256]{1,0:T(8,128)(2,1)}, u32[]{:S(2)}) copy-start(bf16[128,256]{1,0:T(8,128)(2,1)} %param.25) | copy-start | bytes 196612
  567.7 1.0 copy-start.3
  568.7 36.2 %copy-start.13 = (s32[1,64,128]{2,1,0:T(8,128)S(1)}, s32[1,64,128]{2,1,0:T(8,128)}, u32[]{:S(2)}) copy-start(s32[1,64,128]{2,1,0:T(8,128)} %param.31) | copy-start | bytes 98308
  568.7 384.7 %copy-start.11 = (s32[32]{0:T(128)S(1)}, s32[32]{0:T(128)}, u32[]{:S(2)}) copy-start(s32[32]{0:T(128)} %param.28) | copy-start | bytes 388
  570.4 384.8 %copy-start.12 = (s32[256]{0:T(256)S(1)}, s32[256]{0:T(256)}, u32[]{:S(2)}) copy-start(s32[256]{0:T(256)} %param.30) | copy-start | bytes 3076
Sparse Core Ops, SparseCore 0:
  292.5 5.5 reduce-scatter.2
  301.1 13.1 all-gather.1
  462.2 140.1 all-reduce.2
  604.6 348.7 reduce-scatter.4
where the time goes:
time: 970 us; the launch traced here: 965 us
  waiting for transfers between devices  395 us (41%)
  matrix products  334 us (34%)
  blocking collectives  179 us (18%)
  starting transfers between devices  22.6 us (2%)
  between operations  14.3 us (1%)
  other arithmetic  10.4 us (1%)
    reduce_scatter x1, waiting for transfers between devices, per_device(): lax.psum_scatter(hub_grads, 'dom', scatter_dimension=0, tiled=True)  343 us
    dot_general x12, matrix products, scatter_step(): lax.dot_general(chooser, rows_here, (((0,), (0,)), ((), ())), precision=l...  231 us
    all_gather x1, blocking collectives, per_device(): hub_table = lax.all_gather(hub_local, 'dom', axis=0, tiled=True)  179 us
    dot_general x12, matrix products, gather_step(): part_sum = jnp.dot(chooser, table, preferred_element_type=jnp.float32)  79.6 us
    psum x1, waiting for transfers between devices, per_device(): self_total, neighbor_total = lax.psum((self_term, neighbor_term), 'dom')  32 us
  transfers between devices with their start and end apart: 6, of which 4 were waited for; matrix products, arithmetic and copies ran while one was open for 15% of the time, Pallas kernels for 0%

commit v1 on v0

v1 whole, which is shorter than its diff:
```python
import functools

import jax
import jax.numpy as jnp
from jax import lax
from jax.experimental import pallas as pl
from jax.experimental.pallas import tpu as pltpu
from jax.sharding import PartitionSpec as P

MESH = pl.DeviceIdType.MESH
VMEM_SPEC = pl.BlockSpec(memory_space=pltpu.VMEM)
STRIDE = {"y": 16, "x": 4, "z": 1}
CHAINS = (("y", "x", "z"), ("z", "y", "x"), ("x", "z", "y"))
UNIT = 96
BIG = 58 * 2**20


def place():
    dom = lax.axis_index("dom")
    rep = lax.axis_index("rep")
    at = {"y": dom // 16, "x": (dom // 4) % 4, "z": dom % 4}
    return dom, rep, at


def shifted(dom, at, axis, delta):
    there = (at[axis] + delta) % 4
    return dom + (there - at[axis]) * STRIDE[axis]


def greet(dom, rep, at):
    barrier = pltpu.get_barrier_semaphore()
    for axis in "yxz":
        for delta in (1, 2, 3):
            pl.semaphore_signal(
                barrier, inc=1, device_id=(shifted(dom, at, axis, delta), rep), device_id_type=MESH
            )
    pl.semaphore_signal(barrier, inc=1, device_id=(dom, 1 - rep), device_id_type=MESH)
    pl.semaphore_wait(barrier, 10)


class Copies:
    def __init__(self, send, recv):
        self.send, self.recv, self.used, self.open = send, recv, 0, []

    def take(self):
        self.used += 1
        return self.used - 1

    def start(self, number, src, dst, device):
        copy = pltpu.make_async_remote_copy(
            src_ref=src,
            dst_ref=dst,
            send_sem=self.send.at[number],
            recv_sem=self.recv.at[number],
            device_id=device,
            device_id_type=MESH,
        )
        copy.start()
        self.open.append(copy)

    def arrived(self, number, dst, device):
        pltpu.make_async_remote_copy(
            src_ref=dst,
            dst_ref=dst,
            send_sem=self.send.at[number],
            recv_sem=self.recv.at[number],
            device_id=device,
            device_id_type=MESH,
        ).wait_recv()

    def close(self):
        for copy in self.open:
            copy.wait_send()
        self.open = []


def zhalf(ref, chain, half, lead=()):
    two = pl.ds(2 * half, 2)
    if chain == 0:
        return ref.at[lead + (slice(None), slice(None), two)]
    if chain == 1:
        return ref.at[lead + (two,)]
    return ref.at[lead + (slice(None), two)]


N_GATHER = 3 * 12 + 3 * 3 + 9 + 3


def gather_kernel(
    u0, u1, u2, lists, feat, cot, wts, t0, t1, t2, l3, featx, cotx, wtsx, g0, g1, g2, l1, l2, send, recv, local
):
    dom, rep, at = place()
    other = (dom, 1 - rep)
    units, bufs, tables = (u0, u1, u2), (g0, g1, g2), (t0, t1, t2)
    io = Copies(send, recv)
    greet(dom, rep, at)

    mine = []
    for chain in range(3):
        o, m, i = (at[a] for a in CHAINS[chain])
        copy = pltpu.make_async_copy(units[chain], bufs[chain].at[o, m, i], local.at[chain])
        copy.start()
        mine.append(copy)
    own = pltpu.make_async_copy(lists.at[at["y"]], l1.at[at["y"]], local.at[3])
    own.start()

    def block(chain, step, delta):
        o, m, i = (at[a] for a in CHAINS[chain])
        if step == 0:
            return bufs[chain].at[o, m, (i + delta) % 4]
        if step == 1:
            return bufs[chain].at[o, (m + delta) % 4]
        return bufs[chain].at[(o + delta) % 4]

    def half(chain, step, delta, which):
        o, m, i = (at[a] for a in CHAINS[chain])
        if step == 0:
            return bufs[chain].at[o, m, (i + delta) % 4, pl.ds(which * (UNIT // 2), UNIT // 2)]
        if step == 1:
            return bufs[chain].at[o, (m + delta) % 4, pl.ds(which * 2, 2)]
        return bufs[chain].at[(o + delta) % 4, pl.ds(which * 2, 2)]

    list_steps = (
        ("y", lambda j: lists.at[j], lambda j: l1.at[j]),
        ("x", lambda j: l1.at[:, j], lambda j: l2.at[j]),
        ("z", lambda j: l2.at[:, :, j], lambda j: l3.at[j]),
    )
    list_ids = [[io.take() for _ in range(3)] for _ in range(3)]

    def send_lists(step):
        axis, src, dst = list_steps[step]
        for delta in (1, 2, 3):
            there = (at[axis] + delta) % 4
            io.start(
                list_ids[step][delta - 1],
                src(there),
                dst(at[axis]),
                (shifted(dom, at, axis, delta), rep),
            )

    def take_lists(step):
        axis, _, dst = list_steps[step]
        for delta in (1, 2, 3):
            io.arrived(list_ids[step][delta - 1], dst((at[axis] - delta) % 4), other)

    send_lists(0)
    theirs = pl.ds((1 - rep) * 1024, 1024)
    pair_ids = [io.take() for _ in range(3)]
    pairs = ((feat.at[theirs], featx), (cot.at[theirs], cotx), (wts, wtsx))

    swap_ids = [io.take() for _ in range(3)]
    for step in range(3):
        ids = {}
        for chain in range(3):
            axis = CHAINS[chain][2 - step]
            up, down = (shifted(dom, at, axis, 1), rep), (shifted(dom, at, axis, 3), rep)
            if step == 0:
                mine[chain].wait()
            ids[chain] = [io.take() for _ in range(4)]
            io.start(ids[chain][0], block(chain, step, 0), block(chain, step, 0), up)
            io.start(ids[chain][1], block(chain, step, 0), block(chain, step, 0), down)
        if step == 0:
            for number, (src, dst) in zip(pair_ids, pairs):
                io.start(number, src, dst, other)
            own.wait()
        take_lists(step)
        if step < 2:
            axis, src, dst = list_steps[step + 1]
            copy = pltpu.make_async_copy(src(at[axis]), dst(at[axis]), local.at[3])
            copy.start()
            send_lists(step + 1)
            copy.wait()
        for chain in range(3):
            axis = CHAINS[chain][2 - step]
            up, down = (shifted(dom, at, axis, 1), rep), (shifted(dom, at, axis, 3), rep)
            io.arrived(ids[chain][0], block(chain, step, 3), down)
            io.start(ids[chain][2], half(chain, step, 3, 0), half(chain, step, 3, 0), up)
            io.arrived(ids[chain][1], block(chain, step, 1), up)
            io.start(ids[chain][3], half(chain, step, 1, 1), half(chain, step, 1, 1), down)
        for chain in range(3):
            axis = CHAINS[chain][2 - step]
            up, down = (shifted(dom, at, axis, 1), rep), (shifted(dom, at, axis, 3), rep)
            io.arrived(ids[chain][2], half(chain, step, 2, 0), down)
            io.arrived(ids[chain][3], half(chain, step, 2, 1), up)
    keep = []
    for chain in range(3):
        io.start(swap_ids[chain], zhalf(bufs[chain], chain, 1 - rep), tables[chain].at[rep], other)
        copy = pltpu.make_async_copy(
            zhalf(bufs[chain], chain, rep), tables[chain].at[rep], local.at[chain]
        )
        copy.start()
        keep.append(copy)
    for chain in range(3):
        keep[chain].wait()
        io.arrived(swap_ids[chain], tables[chain].at[1 - rep], other)
    for number, (_, dst) in zip(pair_ids, pairs):
        io.arrived(number, dst, other)
    io.close()


TSHAPES = ((2, 4, 4, 2, UNIT, 128), (2, 2, 4, 4, UNIT, 128), (2, 4, 2, 4, UNIT, 128))


def gather_call(units, lists, feat, cot, wts):
    bf = jnp.bfloat16
    return pl.pallas_call(
        gather_kernel,
        out_shape=[jax.ShapeDtypeStruct(s, bf) for s in TSHAPES]
        + [
            jax.ShapeDtypeStruct((4, 4, 4, 1, 128), jnp.int32),
            jax.ShapeDtypeStruct((1024, 128), bf),
            jax.ShapeDtypeStruct((1024, 128), bf),
            jax.ShapeDtypeStruct((256, 256), bf),
        ],
        in_specs=[VMEM_SPEC] * 7,
        out_specs=[VMEM_SPEC] * 7,
        scratch_shapes=[pltpu.VMEM((4, 4, 4, UNIT, 128), bf)] * 3
        + [pltpu.VMEM((4, 4, 4, 1, 128), jnp.int32)] * 2
        + [
            pltpu.SemaphoreType.DMA((N_GATHER,)),
            pltpu.SemaphoreType.DMA((N_GATHER,)),
            pltpu.SemaphoreType.DMA((4,)),
        ],
        compiler_params=pltpu.CompilerParams(
            collective_id=0, has_side_effects=True, vmem_limit_bytes=BIG
        ),
        name="gather_rows",
    )(*units, lists, feat, cot, wts)


def one_hot(picks, counts, rows, base):
    nodes = picks[0].shape[1]
    row = lax.broadcasted_iota(jnp.int16, (rows, nodes), 0)
    table = jnp.zeros((rows, nodes), jnp.bfloat16)
    for pick, count in zip(picks, counts):
        here = jnp.broadcast_to(pick - base, (rows, nodes)).astype(jnp.int16)
        table = jnp.where(
            here == row, jnp.broadcast_to(count.astype(jnp.bfloat16), (rows, nodes)), table
        )
    return table


def ones_at(pick, rows, base=0):
    row = lax.broadcasted_iota(jnp.int32, (rows, pick.shape[1]), 0)
    return jnp.where(pick - base == row, 1.0, 0.0).astype(jnp.bfloat16)


def dot(a, b, over_a=1, over_b=0):
    return lax.dot_general(
        a, b, (((over_a,), (over_b,)), ((), ())), preferred_element_type=jnp.float32
    )


def side_by_side(rep, own, other, axis):
    first = jnp.where(rep == 0, own, other)
    second = jnp.where(rep == 0, other, own)
    return jnp.concatenate([first, second], axis=axis)


def prepare_kernel(counts, raw, rows, feat, picks, mult, units):
    rep = lax.axis_index("rep")
    halo = raw[8:12]
    end = jnp.int32(0)
    sender = jnp.zeros_like(halo)
    before = jnp.zeros_like(halo)
    for p in range(64):
        end = end + counts[0, p]
        passed = halo >= end
        sender = sender + jnp.where(passed, 1, 0)
        before = before + jnp.where(passed, counts[0, p], 0)
    sender = jnp.minimum(sender, 63)
    slot = jnp.clip(halo - before, 0, 127)

    def in_half(p, within, size):
        number = (p >> 2) * 2 + (p & 1)
        return jnp.where(((p & 3) >> 1) == rep, number * size + within, -1)

    hub = raw[12:16]
    local = raw[0:8] - rep * 1024
    local = jnp.where((local >= 0) & (local < 1024), local, -1)
    groups = (local, in_half(sender, slot, 128), in_half(hub >> 5, hub & 31, 32))
    start = 0
    for group in groups:
        size = group.shape[0]
        picks[start : start + size] = group
        for a in range(size):
            total = jnp.zeros((1, group.shape[1]), jnp.float32)
            for b in range(size):
                total = total + jnp.where(group[a : a + 1] == group[b : b + 1], 1.0, 0.0)
            mult[start + a : start + a + 1] = total
        start += size
    chooser = ones_at(rows[...], 2048)
    units[...] = dot(chooser, feat[...], 0, 0).astype(jnp.bfloat16)


def plain(kernel, out_shape, args, name, smem=(), grid=None, scratch=(), in_specs=None, out_specs=None):
    if in_specs is None:
        in_specs = [
            pl.BlockSpec(memory_space=pltpu.SMEM) if n in smem else VMEM_SPEC for n in range(len(args))
        ]
    if out_specs is None:
        out_specs = [VMEM_SPEC] * len(out_shape)
    return pl.pallas_call(
        kernel,
        out_shape=out_shape,
        in_specs=in_specs,
        out_specs=out_specs,
        grid=() if grid is None else grid,
        scratch_shapes=list(scratch),
        compiler_params=pltpu.CompilerParams(vmem_limit_bytes=BIG),
        name=name,
    )(*args)


def chain_index(number):
    y, x, z = number // 8, (number // 2) % 4, number % 2
    return number, z * 16 + y * 4 + x, x * 8 + z * 4 + y


def forward_kernel(picks, mult, t0, t1, t2, lists, feat, featx, out, table):
    rep = lax.axis_index("rep")

    @pl.when(pl.program_id(0) == 0)
    def build():
        for number in range(32):
            i0, i1, i2 = chain_index(number)
            wide = [
                jnp.concatenate([t[0, i], t[1, i]], axis=1) for t, i in ((t0, i0), (t1, i1), (t2, i2))
            ]
            rows = jnp.concatenate([wide[0], wide[1], wide[2][:64]], axis=0)
            y, x, z = number // 8, (number // 2) % 4, number % 2
            chosen = lists[pl.ds(rep * 32 + z * 16 + x * 4 + y, 1)]
            slots = dot(ones_at(chosen, 256), rows, 0, 0)
            table[1024 + number * 128 : 1024 + number * 128 + 128] = slots.astype(jnp.bfloat16)
            table[5120 + number * 32 : 5120 + number * 32 + 32] = wide[2][64:]
        own = feat[pl.ds(pl.multiple_of(rep * 1024, 1024), 1024)]
        table[0:1024] = side_by_side(rep, own, featx[...], 1)

    total = jnp.zeros((picks.shape[1], 256), jnp.float32)
    for first, some, begin, end in ((0, 8, 0, 1024), (8, 4, 1024, 5120), (12, 4, 5120, 6144)):
        chosen = [picks[k : k + 1] for k in range(first, first + some)]
        counts = [mult[k : k + 1] for k in range(first, first + some)]
        for base in range(begin, end, 512):
            total = total + dot(
                one_hot(chosen, counts, 512, base - begin), table[base : base + 512], 0, 0
            )
    out[...] = total


def forward_call(picks, mult, tables, lists, feat, featx):
    full = lambda a: pl.BlockSpec(a.shape, lambda i: (0,) * a.ndim)
    tile = pl.BlockSpec((16, 512), lambda i: (0, i))
    args = [picks, mult, *tables, lists, feat, featx]
    return plain(
        forward_kernel,
        [jax.ShapeDtypeStruct((2048, 256), jnp.float32)],
        args,
        "gather_sum",
        grid=(4,),
        scratch=[pltpu.VMEM((6144, 256), jnp.bfloat16)],
        in_specs=[tile, tile] + [full(a) for a in args[2:]],
        out_specs=[pl.BlockSpec((512, 256), lambda i: (i, 0))],
    )[0]


def middle_kernel(total, totalx, feat, featx, cot, cotx, wts, wtsx, send, agg_own, out_own):
    rep = lax.axis_index("rep")
    mine = pl.ds(pl.multiple_of(rep * 1024, 1024), 1024)
    selfw = side_by_side(rep, wts[0:128], wtsx[0:128], 0)
    nbrw = side_by_side(rep, wts[128:256], wtsx[128:256], 0)
    for step in range(4):
        rows = pl.ds(pl.multiple_of(rep * 1024, 1024) + step * 256, 256)
        part = slice(step * 256, step * 256 + 256)
        features = side_by_side(rep, feat[rows], featx[part], 1)
        cotangent = side_by_side(rep, cot[rows], cotx[part], 1)
        aggregate = ((total[rows] + totalx[part]) * (1.0 / 16.0)).astype(jnp.bfloat16)
        pre_act = dot(features, selfw) + dot(aggregate, nbrw)
        sigmoid = 1.0 / (1.0 + jnp.exp(-pre_act))
        output = (pre_act * sigmoid).astype(jnp.bfloat16)
        slope = sigmoid * (1.0 + pre_act * (1.0 - sigmoid))
        grad = (cotangent.astype(jnp.float32) * slope).astype(jnp.bfloat16)
        send[part, 0:256] = grad
        send[part, 256:384] = jnp.where(rep == 0, aggregate[:, 128:], aggregate[:, :128])
        send[part, 384:512] = jnp.where(rep == 0, output[:, 128:], output[:, :128])
        agg_own[part] = jnp.where(rep == 0, aggregate[:, :128], aggregate[:, 128:])
        out_own[part] = jnp.where(rep == 0, output[:, :128], output[:, 128:])


def backward_kernel(
    picks, mult, lists, feat, sent, got, agg_own, out_own, u0, u1, u2, local, terms, output, grad
):
    rep = lax.axis_index("rep")
    mine = pl.ds(pl.multiple_of(rep * 1024, 1024), 1024)
    theirs = pl.ds(pl.multiple_of((1 - rep) * 1024, 1024), 1024)
    step = pl.program_id(0)

    @pl.when(step == 0)
    def once():
        grad[mine] = sent[:, 0:256]
        grad[theirs] = got[:, 0:256]
        output[mine] = out_own[...]
        output[theirs] = got[:, 384:512]
        selft = dot(feat[...], grad[...], 0, 0)
        nbrt = dot(agg_own[...], sent[:, 0:256], 0, 0) + dot(got[:, 256:384], got[:, 0:256], 0, 0)
        for n, term in enumerate((selft, nbrt)):
            terms[2 * n] = term[:, :128]
            terms[2 * n + 1] = term[:, 128:]

    total = jnp.zeros((768, 256), jnp.float32)
    for begin in range(0, 2048, 256):
        cols = slice(begin, begin + 256)
        parts = []
        for first, some, rows in ((0, 8, 128), (8, 4, 512), (12, 4, 128)):
            chosen = [picks[k : k + 1, cols] for k in range(first, first + some)]
            counts = [mult[k : k + 1, cols] for k in range(first, first + some)]
            parts.append(one_hot(chosen, counts, rows, step * rows))
        total = total + dot(jnp.concatenate(parts, axis=0), grad[cols])
    local[pl.ds(pl.multiple_of(step * 128, 128), 128)] = total[0:128]
    slots = total[128:640].astype(jnp.bfloat16)
    hubs = total[640:768].astype(jnp.bfloat16)
    for k in range(4):
        number = step * 4 + k
        y, x, z = number // 8, (number // 2) % 4, number % 2
        chosen = lists[pl.ds(rep * 32 + z * 16 + x * 4 + y, 1)]
        rows = dot(ones_at(chosen, 256), slots[k * 128 : k * 128 + 128]).astype(jnp.bfloat16)
        i0, i1, i2 = chain_index(number)
        for h in range(2):
            cols = slice(h * 128, h * 128 + 128)
            u0[h, i0] = rows[0:96, cols]
            u1[h, i1] = rows[96:192, cols]
            u2[h, i2, 0:64] = rows[192:256, cols]
            u2[h, i2, 64:96] = hubs[k * 32 : k * 32 + 32, cols]


def backward_call(*args):
    full = lambda a: pl.BlockSpec(a.shape, lambda i: (0,) * len(a.shape))
    shapes = [jax.ShapeDtypeStruct((2, 32, UNIT, 128), jnp.bfloat16)] * 3 + [
        jax.ShapeDtypeStruct((1024, 256), jnp.float32),
        jax.ShapeDtypeStruct((4, 128, 128), jnp.float32),
        jax.ShapeDtypeStruct((2048, 128), jnp.bfloat16),
    ]
    return plain(
        backward_kernel,
        shapes,
        args,
        "scatter_sum",
        grid=(8,),
        scratch=[pltpu.VMEM((2048, 256), jnp.bfloat16)],
        in_specs=[full(a) for a in args],
        out_specs=[full(s) for s in shapes],
    )


N_SCATTER = 3 + 3 * 18 + 18 + 3


def scatter_kernel(u0, u1, u2, terms, r0, r1, r2, sums, *rest):
    bufs = rest[0:3]
    nexts = (rest[3:6], rest[6:9])
    recvs = [rest[9 + 4 * n : 13 + 4 * n] for n in range(9)]
    w1, w2, wb, wc, w3 = rest[45:50]
    send, recv, localsem = rest[50:53]
    dom, rep, at = place()
    other = (dom, 1 - rep)
    units, results = (u0, u1, u2), (r0, r1, r2)
    io = Copies(send, recv)
    greet(dom, rep, at)

    swap_ids = [io.take() for _ in range(3)]
    keep = []
    for chain in range(3):
        io.start(swap_ids[chain], units[chain].at[1 - rep], zhalf(bufs[chain], chain, rep), other)
        copy = pltpu.make_async_copy(
            units[chain].at[rep], zhalf(bufs[chain], chain, rep), localsem.at[chain]
        )
        copy.start()
        keep.append(copy)

    def peers(axis):
        return [
            (delta, (at[axis] + delta) % 4, (shifted(dom, at, axis, delta), rep)) for delta in (1, 2, 3)
        ]

    def reduce_along(axis, src, landing):
        ids = [io.take() for _ in range(3)]
        for delta, there, device in peers(axis):
            io.start(ids[delta - 1], src.at[there], landing.at[delta - 1], device)
        for delta in (1, 2, 3):
            io.arrived(ids[delta - 1], landing.at[delta - 1], other)

    reduce_along("y", terms, w1)
    wb[...] = terms[at["y"]] + w1[0] + w1[1] + w1[2]
    reduce_along("x", wb, w2)
    wc[...] = wb[at["x"]] + w2[0] + w2[1] + w2[2]
    reduce_along("z", wc, w3)
    sums[at["y"], at["x"], at["z"]] = wc[at["z"]] + w3[0] + w3[1] + w3[2]

    def hand_out(axis, ref, start):
        if start:
            ids = [io.take() for _ in range(3)]
            for delta, _, device in peers(axis):
                io.start(ids[delta - 1], ref(at[axis]), ref(at[axis]), device)
            return ids

    def hand_in(axis, ref, ids):
        for delta in (1, 2, 3):
            io.arrived(ids[delta - 1], ref((at[axis] - delta) % 4), other)

    gives = (
        ("z", lambda j: sums.at[at["y"], at["x"], j]),
        ("x", lambda j: sums.at[at["y"], j]),
        ("y", lambda j: sums.at[j]),
    )

    for chain in range(3):
        keep[chain].wait()
        io.arrived(swap_ids[chain], zhalf(bufs[chain], chain, 1 - rep), other)

    now = list(bufs)
    for step in range(3):
        ids = [[io.take() for _ in range(6)] for _ in range(3)]
        lows = pl.ds(0, UNIT // 2) if step == 2 else pl.ds(0, 2)
        highs = pl.ds(UNIT // 2, UNIT // 2) if step == 2 else pl.ds(2, 2)
        loops = (8, 2, 1)[step]

        def ends(chain):
            axis = CHAINS[chain][step]
            i = at[axis]
            up, down = (shifted(dom, at, axis, 1), rep), (shifted(dom, at, axis, 3), rep)
            return i, (i + 1) % 4, (i + 2) % 4, (i + 3) % 4, up, down

        def unit(ref, lead, low, k):
            if step == 0:
                return ref.at[lead + (low * 2 + k // 4, k % 4)]
            if step == 1:
                return ref.at[lead + (low * 2 + k,)]
            return ref.at[lead + (pl.ds(low * (UNIT // 2), UNIT // 2),)]

        for chain in range(3):
            i, above, far, below, up, down = ends(chain)
            data, (from_low, from_high, whole_low, whole_high) = now[chain], recvs[3 * step + chain]
            n = ids[chain]
            io.start(n[0], data.at[far, lows], from_low, up)
            io.start(n[1], data.at[far, highs], from_high, down)
            io.start(n[2], data.at[above, highs], whole_low.at[highs], up)
            io.start(n[3], data.at[below, lows], whole_high.at[lows], down)
        axis, ref = gives[step]
        given = hand_out(axis, ref, True)
        hand_in(axis, ref, given)
        for chain in range(3):
            i, above, far, below, up, down = ends(chain)
            data, (from_low, from_high, whole_low, whole_high) = now[chain], recvs[3 * step + chain]
            n = ids[chain]
            for number, landing, lead, low, target, device in (
                (0, from_low, above, 0, whole_low, up),
                (1, from_high, below, 1, whole_high, down),
            ):
                io.arrived(n[number], landing, other)

                def add(k, carry, landing=landing, lead=lead, low=low):
                    spot = unit(data, (lead,), low, k)
                    came = unit(landing, (), 0, k)
                    spot[...] = (
                        spot[...].astype(jnp.float32) + came[...].astype(jnp.float32)
                    ).astype(jnp.bfloat16)
                    return carry

                lax.fori_loop(0, loops, add, 0)
                part = lows if low == 0 else highs
                io.start(n[4 + number], data.at[lead, part], target.at[part], device)
        for chain in range(3):
            i, above, far, below, up, down = ends(chain)
            data, (from_low, from_high, whole_low, whole_high) = now[chain], recvs[3 * step + chain]
            n = ids[chain]
            io.arrived(n[2], whole_low.at[highs], other)
            io.arrived(n[4], whole_low.at[lows], other)
            io.arrived(n[3], whole_high.at[lows], other)
            io.arrived(n[5], whole_high.at[highs], other)
            target = nexts[step][chain] if step < 2 else results[chain].at[rep]

            def total(k, carry):
                low, rest_k = (k // loops, k % loops)
                value = (
                    unit(data, (i,), low, rest_k)[...].astype(jnp.float32)
                    + unit(whole_low, (), low, rest_k)[...].astype(jnp.float32)
                    + unit(whole_high, (), low, rest_k)[...].astype(jnp.float32)
                )
                spot = unit(target, (), low, rest_k)
                spot[...] = value.astype(target.dtype)
                return carry

            if step == 2:
                target[...] = (
                    data[i].astype(jnp.float32)
                    + whole_low[...].astype(jnp.float32)
                    + whole_high[...].astype(jnp.float32)
                )
            else:
                lax.fori_loop(0, 2 * loops, total, 0)
        if step < 2:
            now = list(nexts[step])
    last = [io.take() for _ in range(3)]
    for chain in range(3):
        io.start(last[chain], results[chain].at[rep], results[chain].at[rep], other)
    for chain in range(3):
        io.arrived(last[chain], results[chain].at[1 - rep], other)
    io.close()


def scatter_call(units, terms):
    bf, f32 = jnp.bfloat16, jnp.float32
    recvs = []
    for lead in ((4, 4), (4,), ()):
        whole = lead + (UNIT, 128)
        half = (whole[0] // 2,) + whole[1:]
        for _ in range(3):
            recvs += [pltpu.VMEM(s, bf) for s in (half, half, whole, whole)]
    return pl.pallas_call(
        scatter_kernel,
        out_shape=[jax.ShapeDtypeStruct((2, UNIT, 128), f32)] * 3
        + [jax.ShapeDtypeStruct((4, 4, 4, 8, 128), f32)],
        in_specs=[VMEM_SPEC] * 4,
        out_specs=[VMEM_SPEC] * 4,
        scratch_shapes=[pltpu.VMEM((4, 4, 4, UNIT, 128), bf)] * 3
        + [pltpu.VMEM((4, 4, UNIT, 128), bf)] * 3
        + [pltpu.VMEM((4, UNIT, 128), bf)] * 3
        + recvs
        + [
            pltpu.VMEM((3, 4, 4, 8, 128), f32),
            pltpu.VMEM((3, 4, 8, 128), f32),
            pltpu.VMEM((4, 4, 8, 128), f32),
            pltpu.VMEM((4, 8, 128), f32),
            pltpu.VMEM((3, 8, 128), f32),
            pltpu.SemaphoreType.DMA((N_SCATTER,)),
            pltpu.SemaphoreType.DMA((N_SCATTER,)),
            pltpu.SemaphoreType.DMA((3,)),
        ],
        compiler_params=pltpu.CompilerParams(
            collective_id=1, has_side_effects=True, vmem_limit_bytes=BIG
        ),
        name="scatter_rows",
    )(*units, terms)


def final_kernel(rows, r0, r1, r2, local, sent, wts, wtsx, keep, give):
    rep = lax.axis_index("rep")
    selfw = side_by_side(rep, wts[0:128], wtsx[0:128], 0)
    nbrw = side_by_side(rep, wts[128:256], wtsx[128:256], 0)
    totals = jnp.concatenate(
        [jnp.concatenate([r[0], r[1]], axis=1) for r in (r0, r1, r2)], axis=0
    )
    high = totals.astype(jnp.bfloat16)
    low = (totals - high.astype(jnp.float32)).astype(jnp.bfloat16)
    for step in range(4):
        part = slice(step * 256, step * 256 + 256)
        chooser = ones_at(rows[...], 256, rep * 1024 + step * 256)
        sums = local[part] + dot(chooser, high) + dot(chooser, low)
        sums = (sums * (1.0 / 16.0)).astype(jnp.bfloat16)
        value = dot(sent[part, 0:256], selfw, 1, 1) + dot(sums, nbrw, 1, 1)
        value = value.astype(jnp.bfloat16)
        keep[part] = jnp.where(rep == 0, value[:, :128], value[:, 128:])
        give[part] = jnp.where(rep == 0, value[:, 128:], value[:, :128])


PAIR = ((0, 1), (1, 0))


def per_device(
    features,
    cotangent,
    self_weight,
    neighbor_weight,
    local_neighbors,
    hub_rows,
    hub_neighbors,
    boundary_rows,
    send_lists,
    received_counts,
    halo_neighbors,
):
    bf, f32 = jnp.bfloat16, jnp.float32
    rep = lax.axis_index("rep")
    raw = jnp.concatenate([local_neighbors, halo_neighbors, hub_neighbors], axis=1).T
    rows = jnp.concatenate([boundary_rows, hub_rows])[None]
    picks, mult, units = plain(
        prepare_kernel,
        [
            jax.ShapeDtypeStruct((16, 2048), jnp.int32),
            jax.ShapeDtypeStruct((16, 2048), f32),
            jax.ShapeDtypeStruct((288, 128), bf),
        ],
        [received_counts, raw, rows, features],
        "prepare",
        smem=(0,),
    )
    weights = jnp.concatenate([self_weight, neighbor_weight], axis=0)
    *tables, lists, featx, cotx, wtsx = gather_call(
        [units[UNIT * c : UNIT * c + UNIT] for c in range(3)],
        send_lists.reshape(4, 4, 4, 1, 128),
        features,
        cotangent,
        weights,
    )
    tables = [t.reshape(2, 32, UNIT, 128) for t in tables]
    lists = lists.reshape(64, 128)
    total = forward_call(picks, mult, tables, lists, features, featx)
    theirs = lax.dynamic_slice_in_dim(total, (1 - rep) * 1024, 1024, 0)
    totalx = lax.ppermute(theirs, "rep", PAIR)
    sent, agg_own, out_own = plain(
        middle_kernel,
        [
            jax.ShapeDtypeStruct((1024, 512), bf),
            jax.ShapeDtypeStruct((1024, 128), bf),
            jax.ShapeDtypeStruct((1024, 128), bf),
        ],
        [total, totalx, features, featx, cotangent, cotx, weights, wtsx],
        "middle",
    )
    got = lax.ppermute(sent, "rep", PAIR)
    u0, u1, u2, local, terms, output = backward_call(
        picks, mult, lists, features, sent, got, agg_own, out_own
    )
    r0, r1, r2, sums = scatter_call(
        [u.reshape(s) for u, s in zip((u0, u1, u2), TSHAPES)], terms.reshape(4, 4, 4, 8, 128)
    )
    keep, give = plain(
        final_kernel,
        [jax.ShapeDtypeStruct((1024, 128), bf)] * 2,
        [rows, r0, r1, r2, local, sent, weights, wtsx],
        "final",
    )
    came = lax.ppermute(give, "rep", PAIR)
    gradient = side_by_side(rep, keep, came, 0)
    sums = sums.reshape(2, 2, 128, 128) * (131072.0**-0.5)
    sums = jnp.concatenate([sums[:, 0], sums[:, 1]], axis=2)
    return output, gradient, sums[0], sums[1]


def solution(mesh):
    return jax.shard_map(
        per_device,
        mesh=mesh,
        in_specs=(
            P("dom", "rep"),
            P("dom", "rep"),
            P("rep", None),
            P("rep", None),
            P("dom", None),
            P("dom"),
            P("dom", None),
            P("dom"),
            P("dom", None, None),
            P("dom", None),
            P("dom", None),
        ),
        out_specs=(P("dom", "rep"), P("dom", "rep"), P("rep", None), P("rep", None)),
        check_vma=False,
    )
```

time: 970 us -> 169 us (0.17)
  the two profiles are of different devices: /device:TPU:0 before, /device:TPU:1 now
where the time goes in v1:
time: 169 us
  Pallas kernels  148 us (88%)
  local copies, waits for them, and re-layouts  7.52 us (4%)
  waiting for transfers between devices  6.32 us (4%)
  other arithmetic  5.8 us (3%)
    pallas_call x1, Pallas kernels, scatter_call(): pl.pallas_call(scatter_kernel, out_shape=[jax.ShapeDtypeStruct((2, UNIT,...  53.8 us
    pallas_call x1, Pallas kernels, gather_call(): pl.pallas_call(gather_kernel, out_shape=[jax.ShapeDtypeStruct(s, bf) for...  48 us
    pallas_call x5, Pallas kernels, plain(): pl.pallas_call(kernel, out_shape=out_shape, in_specs=in_specs, out_specs=...  46.1 us
    unnamed x7, local copies, waits for them, and re-layouts  3.43 us
  transfers between devices with their start and end apart: 3, of which 3 were waited for; matrix products, arithmetic and copies ran while one was open for 0% of the time, Pallas kernels for 0%

profile of v1, /device:TPU:1, one launch (start us, length us, event | category | flops | bytes accessed | tf_op | source)
XLA Modules:
  0.0 168.5 jit_solution(18209981986289895736)
XLA Ops:
  0.6 0.7 pad_add_fusion
  1.3 0.5 broadcast_in_dim.3.rows
  1.9 0.8 constant_dynamic-update-slice_fusion.1
  2.7 1.6 add_bitcast_fusion.raw
  4.3 3.5 %prepare.1 = (s32[16,2048]{1,0:T(8,128)}, f32[16,2048]{1,0:T(8,128)}, bf16[288,128]{1,0:T(8,128)(2,1)}) custom-call(s32[1,64]{1,0:T(1,128)} %counts.1, s32[16,2048]{1,0:T(8,128)} %add_bitcast_fusion.raw, s32[1,288]{1,0:T(1,128)} %broadcast_in_dim.3.rows, bf16[2048,128]{1,0:T(8,128)(2,1)} %feat.9), custom_call_target="tpu_custom_call" | custom-call | tf_op jit(solution)/shard_map/prepare/pallas_call | solution.py:303
  7.8 1.4 fusion.3
  9.2 0.8 constant_dynamic-update-slice_fusion.wts
  10.0 0.0 copy-start
  10.0 0.7 copy-done
  10.7 48.0 %gather_rows.1 = (bf16[2,4,4,2,96,128]{5,4,3,2,1,0:T(8,128)(2,1)}, bf16[2,2,4,4,96,128]{5,4,3,2,1,0:T(8,128)(2,1)}, bf16[2,4,2,4,96,128]{5,4,3,2,1,0:T(8,128)(2,...) custom-call(bf16[96,128]{1,0:T(8,128)(2,1)} %get-tuple-element.62.u0, ...), custom_call_target="tpu_custom_call" | custom-call | tf_op jit(solution)/shard_map/gather_rows/pallas_call | solution.py:206
  58.7 14.2 %gather_sum.1.total = f32[2048,256]{1,0:T(8,128)} custom-call(s32[16,2048]{1,0:T(8,128)} %get-tuple-element.29.picks, f32[16,2048]{1,0:T(8,128)} %get-tuple-element.30.mult, bf16[2,32,96,128]{3,2,1,0:T(8,128)(2,1)} %bitcast.27, bf16[2,32,96,128]{3,2,1,0:T(8,128)(2,1)} %bitcast.28, bf16[2,32,96,128]{3,2,1,0:T(8,128)(2,1)} %bitcast.29, s32[64,128]{1,0:T(8,128)} %bitcast.32, ...), custom_call_target="tpu_custom_call" | custom-call | tf_op jit(solution)/shard_map/gather_sum/pallas_call | solution.py:303
  72.8 1.3 constant_dynamic-slice_fusion
  74.1 0.1 collective-permute-start
  74.3 2.6 %collective-permute-done.totalx = f32[1024,256]{1,0:T(8,128)S(1)} collective-permute-done((f32[1024,256]{1,0:T(8,128)S(1)}, f32[1024,256]{1,0:T(8,128)S(1)}, u32[]{:S(2)}, u32[]{:S(2)}) %collective-permute-start) | collective-permute-done | bytes 1048608 | tf_op jit(solution)/shard_map/ppermute | solution.py:708
  76.9 0.0 copy-start.1
  76.9 1.0 copy-done.1
  77.9 4.3 %middle.1 = (bf16[1024,512]{1,0:T(8,128)(2,1)}, bf16[1024,128]{1,0:T(8,128)(2,1)}, bf16[1024,128]{1,0:T(8,128)(2,1)}) custom-call(f32[2048,256]{1,0:T(8,128)} %gather_sum.1.total, f32[1024,256]{1,0:T(8,128)} %copy-done.1, bf16[2048,128]{1,0:T(8,128)(2,1)} %feat.9, bf16[1024,128]{1,0:T(8,128)(2,1)} %get-tuple-element.36.featx, bf16[2048,128]{1,0:T(8,128)(2,1)} %cot.3, ...), custom_call_target="tpu_custom_call" | custom-call | tf_op jit(solution)/shard_map/middle/pallas_call | solution.py:303
  82.2 0.1 collective-permute-start.1
  82.3 2.7 %collective-permute-done.1.got = bf16[1024,512]{1,0:T(8,128)(2,1)S(1)} collective-permute-done((bf16[1024,512]{1,0:T(8,128)(2,1)}, bf16[1024,512]{1,0:T(8,128)(2,1)S(1)}, u32[]{:S(2)}, u32[]{:S(2)}) %collective-permute-start.1) | collective-permute-done | bytes 1048608 | tf_op jit(solution)/shard_map/ppermute | solution.py:719
  85.0 0.0 copy-start.2
  85.0 1.0 copy-done.2
  86.0 19.6 %scatter_sum.1 = (bf16[2,32,96,128]{3,2,1,0:T(8,128)(2,1)}, bf16[2,32,96,128]{3,2,1,0:T(8,128)(2,1)}, bf16[2,32,96,128]{3,2,1,0:T(8,128)(2,1)}, f32[1024,256]{1,...) custom-call(s32[16,2048]{1,0:T(8,128)} %get-tuple-element.29.picks, f32[16,2048]{1,0:T(8,128)} %get-tuple-element.30.mult, ...), custom_call_target="tpu_custom_call" | custom-call | tf_op jit(solution)/shard_map/scatter_sum/pallas_call | solution.py:303
  105.6 53.8 %scatter_rows.1 = (f32[2,96,128]{2,1,0:T(8,128)}, f32[2,96,128]{2,1,0:T(8,128)}, f32[2,96,128]{2,1,0:T(8,128)}, f32[4,4,4,8,128]{4,3,2,1,0:T(8,128)}) custom-call(bf16[2,4,4,2,96,128]{5,4,3,2,1,0:T(8,128)(2,1)} %bitcast.24, bf16[2,2,4,4,96,128]{5,4,3,2,1,0:T(8,128)(2,1)} %bitcast.25, bf16[2,4,2,4,96,128]{5,4,3,2,1,0:T(8,128)(2,1)} %bitcast.26, ...), custom_call_target="tpu_custom_call" | custom-call | tf_op jit(solution)/shard_map/scatter_rows/pallas_call | solution.py:618
  159.5 1.0 broadcast_multiply_fusion
  160.4 4.5 %final.1 = (bf16[1024,128]{1,0:T(8,128)(2,1)}, bf16[1024,128]{1,0:T(8,128)(2,1)}) custom-call(s32[1,288]{1,0:T(1,128)} %broadcast_in_dim.3.rows, f32[2,96,128]{2,1,0:T(8,128)} %get-tuple-element.47.r0, f32[2,96,128]{2,1,0:T(8,128)} %get-tuple-element.48.r1, f32[2,96,128]{2,1,0:T(8,128)} %get-tuple-element.49.r2, f32[1024,256]{1,0:T(8,128)} %get-tuple-element.50.local, ...), custom_call_target="tpu_custom_call" | custom-call | tf_op jit(solution)/shard_map/final/pallas_call | solution.py:303
  164.9 0.0 collective-permute-start.2
  165.0 0.7 fusion.2
  165.7 1.0 collective-permute-done.2
  166.7 1.0 broadcast_select_fusion.1
  167.7 0.8 pad_maximum_fusion
  (1 shorter events, 0.0 us)
Async XLA Ops:
  10.0 0.7 copy-start
  74.1 2.7 %collective-permute-start = (f32[1024,256]{1,0:T(8,128)S(1)}, f32[1024,256]{1,0:T(8,128)S(1)}, u32[]{:S(2)}, u32[]{:S(2)}) collective-permute-start(f32[1024,256]{1,0:T(8,128)S(1)} %constant_dynamic-slice_fusion), channel_id=1, source_target_pairs={{0,1},{1,0},{2,3},{3,2},{4,5},{5,4},{6,7},{7,6},{8,9},{9,8},{10,11... | collective-permute-start | bytes 3145736 | tf_op jit(solution)/shard_map/ppermute | solution.py:708
  76.9 1.0 copy-start.1
  82.2 2.9 %collective-permute-start.1 = (bf16[1024,512]{1,0:T(8,128)(2,1)}, bf16[1024,512]{1,0:T(8,128)(2,1)S(1)}, u32[]{:S(2)}, u32[]{:S(2)}) collective-permute-start(bf16[1024,512]{1,0:T(8,128)(2,1)} %get-tuple-element.39.sent), channel_id=1, source_target_pairs={{0,1},{1,0},{2,3},{3,2},{4,5},{5,4},{6,7},{7,6},{8,9},{9,8},{10,11... | collective-permute-start | bytes 3145736 | tf_op jit(solution)/shard_map/ppermute | solution.py:719
  85.0 1.0 copy-start.2
  164.9 1.7 %collective-permute-start.2 = (bf16[1024,128]{1,0:T(8,128)(2,1)}, bf16[1024,128]{1,0:T(8,128)(2,1)S(1)}, u32[]{:S(2)}, u32[]{:S(2)}) collective-permute-start(bf16[1024,128]{1,0:T(8,128)(2,1)} %get-tuple-element.52), channel_id=1, source_target_pairs={{0,1},{1,0},{2,3},{3,2},{4,5},{5,4},{6,7},{7,6},{8,9},{9,8},{10,11... | collective-permute-start | bytes 786440 | tf_op jit(solution)/shard_map/ppermute | solution.py:732

commit v2 on v0

v2 whole, which is shorter than its diff:
```python
import functools

import jax
import jax.numpy as jnp
from jax import lax
from jax.experimental import pallas as pl
from jax.experimental.pallas import tpu as pltpu
from jax.sharding import PartitionSpec as P

MESH = pl.DeviceIdType.MESH
VMEM_SPEC = pl.BlockSpec(memory_space=pltpu.VMEM)
STRIDE = {"y": 16, "x": 4, "z": 1}
CHAINS = (("y", "x", "z"), ("z", "y", "x"), ("x", "z", "y"))
UNIT = 96
BIG = 58 * 2**20


def place():
    dom = lax.axis_index("dom")
    rep = lax.axis_index("rep")
    at = {"y": dom // 16, "x": (dom // 4) % 4, "z": dom % 4}
    return dom, rep, at


def shifted(dom, at, axis, delta):
    there = (at[axis] + delta) % 4
    return dom + (there - at[axis]) * STRIDE[axis]


def signal_all(dom, rep, at):
    barrier = pltpu.get_barrier_semaphore()
    for axis in "yxz":
        for delta in (1, 2, 3):
            pl.semaphore_signal(
                barrier, inc=1, device_id=(shifted(dom, at, axis, delta), rep), device_id_type=MESH
            )
    pl.semaphore_signal(barrier, inc=1, device_id=(dom, 1 - rep), device_id_type=MESH)


class Copies:
    def __init__(self, send, recv):
        self.send, self.recv, self.used, self.open = send, recv, 0, []

    def take(self):
        self.used += 1
        return self.used - 1

    def start(self, number, src, dst, device):
        copy = pltpu.make_async_remote_copy(
            src_ref=src,
            dst_ref=dst,
            send_sem=self.send.at[number],
            recv_sem=self.recv.at[number],
            device_id=device,
            device_id_type=MESH,
        )
        copy.start()
        self.open.append(copy)

    def arrived(self, number, dst, device):
        pltpu.make_async_remote_copy(
            src_ref=dst,
            dst_ref=dst,
            send_sem=self.send.at[number],
            recv_sem=self.recv.at[number],
            device_id=device,
            device_id_type=MESH,
        ).wait_recv()

    def close(self):
        for copy in self.open:
            copy.wait_send()
        self.open = []


def one_hot(picks, counts, rows, base):
    nodes = picks[0].shape[1]
    row = lax.broadcasted_iota(jnp.int16, (rows, nodes), 0)
    table = jnp.zeros((rows, nodes), jnp.bfloat16)
    for pick, count in zip(picks, counts):
        here = jnp.broadcast_to(pick - base, (rows, nodes)).astype(jnp.int16)
        table = jnp.where(
            here == row, jnp.broadcast_to(count.astype(jnp.bfloat16), (rows, nodes)), table
        )
    return table


def ones_at(pick, rows, base=0):
    row = lax.broadcasted_iota(jnp.int32, (rows, pick.shape[1]), 0)
    return jnp.where(pick - base == row, 1.0, 0.0).astype(jnp.bfloat16)


def dot(a, b, over_a=1, over_b=0):
    return lax.dot_general(
        a, b, (((over_a,), (over_b,)), ((), ())), preferred_element_type=jnp.float32
    )


def side_by_side(rep, own, other, axis):
    first = jnp.where(rep == 0, own, other)
    second = jnp.where(rep == 0, other, own)
    return jnp.concatenate([first, second], axis=axis)


NORM = 131072.0**-0.5
N_COPIES = 420
PIECES = (0, 3, 1, 2)
ORDER = (2, 1, 3, 0)
BF, F32, I32 = jnp.bfloat16, jnp.float32, jnp.int32
SCRATCH = (
    [("g%d" % c, (4, 4, 4, UNIT, 128), BF) for c in range(3)]
    + [("x0", (4, 4, 2, UNIT, 128), BF), ("x1", (2, 4, 4, UNIT, 128), BF), ("x2", (4, 2, 4, UNIT, 128), BF)]
    + [("give0", (4, 4, 2, UNIT, 128), BF), ("give1", (2, 4, 4, UNIT, 128), BF)]
    + [("give2", (4, 2, 4, UNIT, 128), BF)]
    + [(name, (4, 4, 4, 1, 128), I32) for name in ("l1", "l2", "l3")]
    + [("featx", (1024, 128), BF), ("cotx", (1024, 128), BF), ("wsx", (128, 256), BF), ("wnx", (128, 256), BF)]
    + [("chooser", (2048, 288), BF), ("units", (288, 128), BF)]
    + [("picks", (16, 2048), I32), ("mult", (16, 2048), F32), ("table", (6144, 256), BF)]
    + [("total", (2048, 256), F32), ("totalx", (1024, 256), F32), ("grad", (2048, 256), BF)]
    + [("agg_send", (1024, 128), BF), ("out_send", (1024, 128), BF), ("agg_cols", (2048, 128), BF)]
    + [("terms", (4, 4, 4, 8, 128), F32), ("sums", (4, 4, 4, 8, 128), F32)]
    + [("local_sums", (2048, 256), BF)]
    + [("w1", (3, 4, 4, 8, 128), F32), ("w2", (3, 4, 8, 128), F32), ("wb", (4, 4, 8, 128), F32)]
    + [("wc", (4, 8, 128), F32), ("w3", (3, 8, 128), F32)]
    + [("r%d" % c, (2, UNIT, 128), F32) for c in range(3)]
    + [("whole%d" % c, (4, 4, 4, UNIT, 128), BF) for c in range(3)]
    + [("first%d" % c, (4, 4, UNIT, 128), BF) for c in range(3)]
    + [("second%d" % c, (4, UNIT, 128), BF) for c in range(3)]
    + [
        ("%s%d%d" % (stage, c, n), lead + ((shape[0] // 2,) + shape[1:] if n < 2 else shape), BF)
        for stage, lead, shape in (
            ("outer", (4,), (4, UNIT, 128)),
            ("middle", (), (4, UNIT, 128)),
            ("inner", (), (UNIT, 128)),
        )
        for c in range(3)
        for n in range(4)
    ]
)


def layer_kernel(*refs):
    (features, cotangent, self_weight, neighbor_weight, raw, brows, hrows, lists, counts) = refs[:9]
    output, gradient, grad_self, grad_neighbor = refs[9:13]
    named = {name: ref for (name, _, _), ref in zip(SCRATCH, refs[13:])}
    send, recv, local = refs[13 + len(SCRATCH) :]
    g0, g1, g2 = bufs = [named["g%d" % c] for c in range(3)]
    x0, x1, x2 = [named["x%d" % c] for c in range(3)]
    give0, give1, give2 = [named["give%d" % c] for c in range(3)]
    l1, l2, l3 = named["l1"], named["l2"], named["l3"]
    featx, cotx, wsx, wnx = named["featx"], named["cotx"], named["wsx"], named["wnx"]
    chooser, units, picks, mult = named["chooser"], named["units"], named["picks"], named["mult"]
    table, total, totalx, grad = named["table"], named["total"], named["totalx"], named["grad"]
    agg_send, out_send, agg_cols = named["agg_send"], named["out_send"], named["agg_cols"]
    terms, sums, local_sums = named["terms"], named["sums"], named["local_sums"]
    w1, w2, wb, wc, w3 = (named[name] for name in ("w1", "w2", "wb", "wc", "w3"))
    results = [named["r%d" % c] for c in range(3)]
    wholes = [named["whole%d" % c] for c in range(3)]
    firsts = [named["first%d" % c] for c in range(3)]
    seconds = [named["second%d" % c] for c in range(3)]
    outer_recv, middle_recv, inner_recv = (
        [[named["%s%d%d" % (stage, c, n)] for n in range(4)] for c in range(3)]
        for stage in ("outer", "middle", "inner")
    )
    dom, rep, at = place()
    other = (dom, 1 - rep)
    io = Copies(send, recv)
    signal_all(dom, rep, at)
    chooser[:, 0:256] = ones_at(brows[...], 2048)
    chooser[:, 256:288] = ones_at(hrows[...], 2048)
    units[...] = dot(chooser[...], features[...], 0, 0).astype(BF)
    pl.semaphore_wait(pltpu.get_barrier_semaphore(), 10)

    def prepare():
        halo = raw[8:12]
        end = jnp.int32(0)
        sender = jnp.zeros_like(halo)
        before = jnp.zeros_like(halo)
        for p in range(64):
            end = end + counts[0, p]
            passed = halo >= end
            sender = sender + jnp.where(passed, 1, 0)
            before = before + jnp.where(passed, counts[0, p], 0)
        sender = jnp.minimum(sender, 63)
        slot = jnp.clip(halo - before, 0, 127)

        def in_half(p, within, size):
            number = (p >> 2) * 2 + (p & 1)
            return jnp.where(((p & 3) >> 1) == rep, number * size + within, -1)

        hub = raw[12:16]
        local = raw[0:8] - rep * 1024
        local = jnp.where((local >= 0) & (local < 1024), local, -1)
        groups = (local, in_half(sender, slot, 128), in_half(hub >> 5, hub & 31, 32))
        start = 0
        for group in groups:
            size = group.shape[0]
            picks[start : start + size] = group
            for a in range(size):
                total = jnp.zeros((1, group.shape[1]), jnp.float32)
                for b in range(size):
                    total = total + jnp.where(group[a : a + 1] == group[b : b + 1], 1.0, 0.0)
                mult[start + a : start + a + 1] = total
            start += size

    def local_gather(tile):
        cols = slice(tile * 512, tile * 512 + 512)
        chosen = [picks[k : k + 1, cols] for k in range(8)]
        counts_of = [mult[k : k + 1, cols] for k in range(8)]
        total[cols] = dot(one_hot(chosen, counts_of, 512, 0), table[0:512], 0, 0) + dot(
            one_hot(chosen, counts_of, 512, 512), table[512:1024], 0, 0
        )

    coords = [tuple(at[a] for a in CHAINS[chain]) for chain in range(3)]
    ways = [
        [
            ((shifted(dom, at, a, 1), rep), (shifted(dom, at, a, 3), rep))
            for a in CHAINS[chain]
        ]
        for chain in range(3)
    ]

    inner_ids = [[io.take() for _ in range(4)] for _ in range(3)]
    mine = []
    for chain in range(3):
        o, m, i = coords[chain]
        up, down = ways[chain][2]
        io.start(inner_ids[chain][0], units.at[pl.ds(chain * UNIT, UNIT)], bufs[chain].at[o, m, i], up)
        io.start(inner_ids[chain][1], units.at[pl.ds(chain * UNIT, UNIT)], bufs[chain].at[o, m, i], down)
        copy = pltpu.make_async_copy(units.at[pl.ds(chain * UNIT, UNIT)], bufs[chain].at[o, m, i], local.at[chain])
        copy.start()
        mine.append(copy)

    list_steps = (
        ("y", lambda j: lists.at[j], lambda j: l1.at[j]),
        ("x", lambda j: l1.at[:, j], lambda j: l2.at[j]),
        ("z", lambda j: l2.at[:, :, j], lambda j: l3.at[j]),
    )
    list_ids = [[io.take() for _ in range(3)] for _ in range(3)]

    def send_lists(step):
        axis, src, dst = list_steps[step]
        for delta in (1, 2, 3):
            there = (at[axis] + delta) % 4
            io.start(
                list_ids[step][delta - 1],
                src(there),
                dst(at[axis]),
                (shifted(dom, at, axis, delta), rep),
            )
        copy = pltpu.make_async_copy(src(at[axis]), dst(at[axis]), local.at[3])
        copy.start()
        return copy

    def take_lists(step, copy):
        axis, _, dst = list_steps[step]
        copy.wait()
        for delta in (1, 2, 3):
            io.arrived(list_ids[step][delta - 1], dst((at[axis] - delta) % 4), other)

    theirs = pl.ds(pl.multiple_of((1 - rep) * 1024, 1024), 1024)
    pairs = (
        (features.at[theirs], featx),
        (self_weight, wsx),
        (neighbor_weight, wnx),
        (cotangent.at[theirs], cotx),
    )
    pair_ids = [io.take() for _ in pairs]
    for number, (src, dst) in zip(pair_ids, pairs):
        io.start(number, src, dst, other)
    listed = send_lists(0)
    prepare()

    swap0, swap1, swap2 = io.used, io.used + 16, io.used + 24
    io.used += 32

    def swap(chain, o, m):
        if chain == 0:
            pltpu.make_async_remote_copy(
                src_ref=g0.at[o, m, pl.ds(2 * (1 - rep), 2)],
                dst_ref=x0.at[o, m],
                send_sem=send.at[swap0 + o * 4 + m],
                recv_sem=recv.at[swap0 + o * 4 + m],
                device_id=other,
                device_id_type=MESH,
            ).start()
            return
        z = o if chain == 1 else m

        @pl.when(z // 2 != rep)
        def _():
            if chain == 1:
                number, dst = swap1 + (o % 2) * 4 + m, x1.at[o % 2, m]
            else:
                number, dst = swap2 + o * 2 + m % 2, x2.at[o, m % 2]
            pltpu.make_async_remote_copy(
                src_ref=bufs[chain].at[o, m],
                dst_ref=dst,
                send_sem=send.at[number],
                recv_sem=recv.at[number],
                device_id=other,
                device_id_type=MESH,
            ).start()

    middle_ids = [[io.take() for _ in range(4)] for _ in range(3)]
    outer_ids = [[[io.take() for _ in range(4)] for _ in range(4)] for _ in range(3)]

    def spread(chain, piece):
        o, m, _ = coords[chain]
        up, down = ways[chain][0]
        block = bufs[chain].at[o, (m + piece) % 4]
        ids = outer_ids[chain][piece]
        io.start(ids[0], block, block, up)
        io.start(ids[1], block, block, down)
        swap(chain, o, (m + piece) % 4)

    def pass_on(chain, ids, from_down, from_up, half, up, down):
        io.arrived(ids[0], from_down, down)
        io.start(ids[2], half(from_down, 0), half(from_down, 0), up)
        io.arrived(ids[1], from_up, up)
        io.start(ids[3], half(from_up, 1), half(from_up, 1), down)

    def rows_half(ref, which):
        return ref.at[pl.ds(which * (UNIT // 2), UNIT // 2)]

    def units_half(ref, which):
        return ref.at[pl.ds(which * 2, 2)]


    def inner_pass():
        for chain in range(3):
            o, m, i = coords[chain]
            up, down = ways[chain][2]
            buf = bufs[chain]
            pass_on(
                chain,
                inner_ids[chain],
                buf.at[o, m, (i + 3) % 4],
                buf.at[o, m, (i + 1) % 4],
                rows_half,
                up,
                down,
            )

    def inner_end():
        for chain in range(3):
            o, m, i = coords[chain]
            up, down = ways[chain][2]
            far = bufs[chain].at[o, m, (i + 2) % 4]
            mine[chain].wait()
            io.arrived(inner_ids[chain][2], rows_half(far, 0), down)
            io.arrived(inner_ids[chain][3], rows_half(far, 1), up)
            up, down = ways[chain][1]
            block = bufs[chain].at[o, m]
            io.start(middle_ids[chain][0], block, block, up)
            io.start(middle_ids[chain][1], block, block, down)
            spread(chain, 0)

    def middle_pass():
        for chain in range(3):
            o, m, i = coords[chain]
            up, down = ways[chain][1]
            buf = bufs[chain]
            pass_on(
                chain,
                middle_ids[chain],
                buf.at[o, (m + 3) % 4],
                buf.at[o, (m + 1) % 4],
                units_half,
                up,
                down,
            )
            spread(chain, 3)
            spread(chain, 1)

    def middle_end():
        for chain in range(3):
            o, m, i = coords[chain]
            up, down = ways[chain][1]
            far = bufs[chain].at[o, (m + 2) % 4]
            io.arrived(middle_ids[chain][2], units_half(far, 0), down)
            io.arrived(middle_ids[chain][3], units_half(far, 1), up)
            spread(chain, 2)

    def spread_pass(piece):
        for chain in range(3):
            o, m, i = coords[chain]
            up, down = ways[chain][0]
            buf, at_m = bufs[chain], (m + piece) % 4
            pass_on(
                chain,
                outer_ids[chain][piece],
                buf.at[(o + 3) % 4, at_m],
                buf.at[(o + 1) % 4, at_m],
                units_half,
                up,
                down,
            )
            swap(chain, (o + 3) % 4, at_m)
            swap(chain, (o + 1) % 4, at_m)

    def spread_end(piece):
        for chain in range(3):
            o, m, i = coords[chain]
            up, down = ways[chain][0]
            far = bufs[chain].at[(o + 2) % 4, (m + piece) % 4]
            io.arrived(outer_ids[chain][piece][2], units_half(far, 0), down)
            io.arrived(outer_ids[chain][piece][3], units_half(far, 1), up)
            swap(chain, (o + 2) % 4, (m + piece) % 4)

    inner_pass()
    inner_end()
    take_lists(0, listed)
    listed = send_lists(1)
    for number, (_, dst) in zip(pair_ids, pairs):
        io.arrived(number, dst, other)
    own_rows = pl.ds(pl.multiple_of(rep * 1024, 1024), 1024)
    table[0:1024] = side_by_side(rep, features[own_rows], featx[...], 1)
    local_gather(0)
    middle_pass()
    take_lists(1, listed)
    listed = send_lists(2)
    spread_pass(0)
    local_gather(1)
    middle_end()
    spread_end(0)
    spread_pass(3)
    local_gather(2)
    spread_pass(1)
    spread_end(3)
    local_gather(3)
    spread_pass(2)
    take_lists(2, listed)
    spread_end(1)
    spread_end(2)

    def settle(number, ref):
        copy = pltpu.make_async_remote_copy(
            src_ref=ref,
            dst_ref=ref,
            send_sem=send.at[number],
            recv_sem=recv.at[number],
            device_id=other,
            device_id_type=MESH,
        )
        copy.wait_recv()
        copy.wait_send()

    for a in range(4):
        for b in range(4):
            settle(swap0 + a * 4 + b, x0.at[a, b])
        for b in range(2):
            settle(swap1 + b * 4 + a, x1.at[b, a])
            settle(swap2 + a * 2 + b, x2.at[a, b])

    def select(number, carry):
        y, x, z = number // 8, (number // 2) % 4, number % 2
        zz = 2 * rep + z
        wide = [
            side_by_side(rep, own, came, 1)
            for own, came in (
                (g0[y, x, zz], x0[y, x, z]),
                (g1[zz, y, x], x1[z, y, x]),
                (g2[x, zz, y], x2[x, z, y]),
            )
        ]
        rows = jnp.concatenate([wide[0], wide[1], wide[2][:64]], axis=0)
        slots = dot(ones_at(l3[zz, x, y], 256), rows, 0, 0)
        table[pl.ds(pl.multiple_of(1024 + number * 128, 128), 128)] = slots.astype(jnp.bfloat16)
        table[pl.ds(pl.multiple_of(5120 + number * 32, 32), 32)] = wide[2][64:]
        return carry

    lax.fori_loop(0, 32, select, 0)

    def gather_tile(tile):
        cols = pl.ds(pl.multiple_of(tile * 512, 512), 512)
        value = total[cols]
        for first, some, begin, end in ((8, 4, 1024, 5120), (12, 4, 5120, 6144)):
            chosen = [picks[k : k + 1, cols] for k in range(first, first + some)]
            counts_of = [mult[k : k + 1, cols] for k in range(first, first + some)]
            for base in range(begin, end, 512):
                value = value + dot(
                    one_hot(chosen, counts_of, 512, base - begin), table[base : base + 512], 0, 0
                )
        total[cols] = value

    sums_at = io.used
    io.used += 2

    def sum_copy(k, tile):
        cols = pl.ds(pl.multiple_of(tile * 512, 512), 512)
        return pltpu.make_async_remote_copy(
            src_ref=total.at[cols],
            dst_ref=totalx.at[pl.ds(pl.multiple_of(k * 512, 512), 512)],
            send_sem=send.at[sums_at + k],
            recv_sem=recv.at[sums_at + k],
            device_id=other,
            device_id_type=MESH,
        )

    def gather_theirs(k, carry):
        gather_tile((1 - rep) * 2 + k)
        sum_copy(k, (1 - rep) * 2 + k).start()
        return carry

    def gather_mine(k, carry):
        gather_tile(rep * 2 + k)
        return carry

    lax.fori_loop(0, 2, gather_theirs, 0)
    lax.fori_loop(0, 2, gather_mine, 0)

    selfw = side_by_side(rep, self_weight[...], wsx[...], 0)
    nbrw = side_by_side(rep, neighbor_weight[...], wnx[...], 0)
    grad_ids = [[io.take() for _ in range(3)] for _ in range(2)]
    for step in range(4):
        if step % 2 == 0:
            sum_copy(step // 2, (1 - rep) * 2 + step // 2).wait_recv()
        rows = pl.ds(pl.multiple_of(rep * 1024 + step * 256, 256), 256)
        part = slice(step * 256, step * 256 + 256)
        wide = side_by_side(rep, features[rows], featx[part], 1)
        cotan = side_by_side(rep, cotangent[rows], cotx[part], 1)
        aggregate = ((total[rows] + totalx[part]) * (1.0 / 16.0)).astype(jnp.bfloat16)
        pre_act = dot(wide, selfw) + dot(aggregate, nbrw)
        sigmoid = 1.0 / (1.0 + jnp.exp(-pre_act))
        result = (pre_act * sigmoid).astype(jnp.bfloat16)
        slope = sigmoid * (1.0 + pre_act * (1.0 - sigmoid))
        grad[rows] = (cotan.astype(jnp.float32) * slope).astype(jnp.bfloat16)
        agg_send[part] = jnp.where(rep == 0, aggregate[:, 128:], aggregate[:, :128])
        out_send[part] = jnp.where(rep == 0, result[:, 128:], result[:, :128])
        agg_cols[rows] = jnp.where(rep == 0, aggregate[:, :128], aggregate[:, 128:])
        output[rows] = jnp.where(rep == 0, result[:, :128], result[:, 128:])
        if step % 2 == 1:
            n = grad_ids[step // 2]
            tall = pl.ds(pl.multiple_of(rep * 1024 + (step // 2) * 512, 512), 512)
            flat = pl.ds((step // 2) * 512, 512)
            io.start(n[0], grad.at[tall], grad.at[tall], other)
            io.start(n[1], agg_send.at[flat], agg_cols.at[tall], other)
            io.start(n[2], out_send.at[flat], output.at[tall], other)
    for k in range(2):
        sum_copy(k, (1 - rep) * 2 + k).wait_send()

    own_terms = (
        dot(features[own_rows], grad[own_rows], 0, 0),
        dot(agg_cols[own_rows], grad[own_rows], 0, 0),
    )
    for k in range(2):
        tall = pl.ds(pl.multiple_of((1 - rep) * 1024 + k * 512, 512), 512)
        io.arrived(grad_ids[k][0], grad.at[tall], other)
        io.arrived(grad_ids[k][1], agg_cols.at[tall], other)
    for n, (mine_term, data) in enumerate(zip(own_terms, (features, agg_cols))):
        term = mine_term + dot(data[theirs], grad[theirs], 0, 0)
        for h in range(2):
            for b in range(16):
                terms[2 * n + h, b // 4, b % 4] = term[b * 8 : b * 8 + 8, h * 128 : h * 128 + 128]

    def scatter_step(step, carry):
        sums_of = jnp.zeros((640, 256), jnp.float32)
        for begin in range(0, 2048, 256):
            cols = slice(begin, begin + 256)
            parts = []
            for first, some, rows in ((8, 4, 512), (12, 4, 128)):
                chosen = [picks[k : k + 1, cols] for k in range(first, first + some)]
                counts_of = [mult[k : k + 1, cols] for k in range(first, first + some)]
                parts.append(one_hot(chosen, counts_of, rows, step * rows))
            sums_of = sums_of + dot(jnp.concatenate(parts, axis=0), grad[cols])
        slots = sums_of[0:512].astype(jnp.bfloat16)
        hubs = sums_of[512:640].astype(jnp.bfloat16)
        for k in range(4):
            y, x, z = step // 2, (step % 2) * 2 + k // 2, k % 2
            zz = 2 * rep + z
            rows = dot(ones_at(l3[zz, x, y], 256), slots[k * 128 : k * 128 + 128])
            rows = rows.astype(jnp.bfloat16)
            rows = jnp.concatenate([rows, hubs[k * 32 : k * 32 + 32]], axis=0)
            keep = jnp.where(rep == 0, rows[:, :128], rows[:, 128:])
            give = jnp.where(rep == 0, rows[:, 128:], rows[:, :128])
            wholes[0][y, x, zz], give0[y, x, z] = keep[0:96], give[0:96]
            wholes[1][zz, y, x], give1[z, y, x] = keep[96:192], give[96:192]
            wholes[2][x, zz, y], give2[x, z, y] = keep[192:288], give[192:288]
        return carry

    def output_done():
        for k in range(2):
            tall = pl.ds(pl.multiple_of((1 - rep) * 1024 + k * 512, 512), 512)
            io.arrived(grad_ids[k][2], output.at[tall], other)

    def trade(axis, src, dst):
        ids = [io.take() for _ in range(3)]
        for delta in (1, 2, 3):
            device = (shifted(dom, at, axis, delta), rep)
            io.start(ids[delta - 1], src(delta), dst(delta), device)
        return ids

    def traded(ids, dst):
        for delta in (1, 2, 3):
            io.arrived(ids[delta - 1], dst(delta), other)

    def reduce_start(axis, src, landing):
        return trade(axis, lambda d: src.at[(at[axis] + d) % 4], lambda d: landing.at[d - 1])

    def reduce_end(ids, src, axis, landing):
        traded(ids, lambda d: landing.at[d - 1])
        return src[at[axis]] + landing[0] + landing[1] + landing[2]

    def give_start(axis, ref):
        return trade(axis, lambda d: ref(at[axis]), lambda d: ref(at[axis]))

    def give_end(ids, axis, ref):
        traded(ids, lambda d: ref((at[axis] - d) % 4))

    gives = {
        "z": lambda j: sums.at[at["y"], at["x"], j],
        "x": lambda j: sums.at[at["y"], j],
        "y": lambda j: sums.at[j],
    }

    swap_ids = [[io.take() for _ in range(4)] for _ in range(3)]

    def swap_refs(chain, piece, half):
        m = (coords[chain][1] + piece) % 4
        span = pl.ds(2 * half, 2)
        if chain == 0:
            return give0.at[:, m], wholes[0].at[:, m, span]
        if chain == 1:
            return give1.at[:, m], wholes[1].at[span, m]
        return give2.at[:, m % 2], wholes[2].at[:, m]

    def remote(number, src, dst):
        return pltpu.make_async_remote_copy(
            src_ref=src,
            dst_ref=dst,
            send_sem=send.at[number],
            recv_sem=recv.at[number],
            device_id=other,
            device_id_type=MESH,
        )

    def swap_start(chain, piece):
        number = swap_ids[chain][piece]
        src, dst = swap_refs(chain, piece, rep)

        def go():
            remote(number, src, dst).start()

        if chain == 2:
            pl.when((coords[2][1] + piece) % 4 // 2 == rep)(go)
        else:
            go()

    def swap_end(chain, piece):
        number = swap_ids[chain][piece]
        src, dst = swap_refs(chain, piece, rep)
        _, came = swap_refs(chain, piece, 1 - rep)

        def kept():
            remote(number, src, dst).wait_send()

        def got():
            remote(number, came, came).wait_recv()

        if chain == 2:
            here = (coords[2][1] + piece) % 4 // 2 == rep
            pl.when(here)(kept)
            pl.when(jnp.logical_not(here))(got)
        else:
            kept()
            got()


    weigh = reduce_start("y", terms, w1)
    lax.fori_loop(0, 8, scatter_step, 0)
    for piece in ORDER:
        for chain in range(3):
            swap_start(chain, piece)

    outer_ids = [[[io.take() for _ in range(6)] for _ in range(4)] for _ in range(3)]
    middle_ids = [[io.take() for _ in range(6)] for _ in range(3)]
    inner_ids = [[io.take() for _ in range(6)] for _ in range(3)]
    low2, high2 = pl.ds(0, 2), pl.ds(2, 2)
    lowr, highr = pl.ds(0, UNIT // 2), pl.ds(UNIT // 2, UNIT // 2)

    def add_into(spot, came):
        spot[...] = (spot[...].astype(jnp.float32) + came[...].astype(jnp.float32)).astype(jnp.bfloat16)

    def three(a, b, c):
        return a[...].astype(jnp.float32) + b[...].astype(jnp.float32) + c[...].astype(jnp.float32)

    def outer_start(piece):
        for chain in range(3):
            swap_end(chain, piece)
            o, m, i = coords[chain]
            up, down = ways[chain][0]
            data, m = wholes[chain], (m + piece) % 4
            from_low, from_high, whole_low, whole_high = (r.at[piece] for r in outer_recv[chain])
            n = outer_ids[chain][piece]
            io.start(n[0], data.at[(o + 2) % 4, m, low2], from_low, up)
            io.start(n[1], data.at[(o + 2) % 4, m, high2], from_high, down)
            io.start(n[2], data.at[(o + 1) % 4, m, high2], whole_low.at[high2], up)
            io.start(n[3], data.at[(o + 3) % 4, m, low2], whole_high.at[low2], down)

    def outer_pass(piece):
        for chain in range(3):
            o, m, i = coords[chain]
            up, down = ways[chain][0]
            data, m = wholes[chain], (m + piece) % 4
            from_low, from_high, whole_low, whole_high = (r.at[piece] for r in outer_recv[chain])
            n = outer_ids[chain][piece]
            io.arrived(n[0], from_low, other)
            for k in range(2):
                add_into(data.at[(o + 1) % 4, m, k], from_low.at[k])
            io.start(n[4], data.at[(o + 1) % 4, m, low2], whole_low.at[low2], up)
            io.arrived(n[1], from_high, other)
            for k in range(2):
                add_into(data.at[(o + 3) % 4, m, 2 + k], from_high.at[k])
            io.start(n[5], data.at[(o + 3) % 4, m, high2], whole_high.at[high2], down)

    def outer_end(piece):
        for chain in range(3):
            o, m, i = coords[chain]
            data, target = wholes[chain], firsts[chain].at[piece]
            _, _, whole_low, whole_high = (r.at[piece] for r in outer_recv[chain])
            n = outer_ids[chain][piece]
            io.arrived(n[2], whole_low.at[high2], other)
            io.arrived(n[3], whole_high.at[low2], other)
            io.arrived(n[4], whole_low.at[low2], other)
            io.arrived(n[5], whole_high.at[high2], other)
            for k in range(4):
                target[k] = three(
                    data.at[o, (m + piece) % 4, k], whole_low.at[k], whole_high.at[k]
                ).astype(jnp.bfloat16)
            up, down = ways[chain][1]
            from_low, from_high, whole_low, whole_high = middle_recv[chain]
            n = middle_ids[chain]
            if piece == 2:
                io.start(n[0], target.at[low2], from_low, up)
                io.start(n[1], target.at[high2], from_high, down)
            if piece == 1:
                io.start(n[2], target.at[high2], whole_low.at[high2], up)
            if piece == 3:
                io.start(n[3], target.at[low2], whole_high.at[low2], down)


    local_ids = [io.take() for _ in range(4)]

    def local_scatter(part):
        value = jnp.zeros((256, 256), jnp.float32)
        for begin in range(0, 2048, 512):
            cols = slice(begin, begin + 512)
            chosen = [picks[k : k + 1, cols] for k in range(8)]
            counts_of = [mult[k : k + 1, cols] for k in range(8)]
            value = value + dot(one_hot(chosen, counts_of, 256, part * 256), grad[cols])
        rows = pl.ds(pl.multiple_of(rep * 1024 + part * 256, 256), 256)
        local_sums[rows] = (value * (1.0 / 16.0)).astype(jnp.bfloat16)
        io.start(local_ids[part], local_sums.at[rows], local_sums.at[rows], other)

    def products(half):
        if half == 0:
            for part in range(4):
                rows = pl.ds(pl.multiple_of((1 - rep) * 1024 + part * 256, 256), 256)
                io.arrived(local_ids[part], local_sums.at[rows], other)
        for begin in range(half * 1024, half * 1024 + 1024, 512):
            rows = slice(begin, begin + 512)
            total[rows, 0:128] = dot(grad[rows], self_weight[...], 1, 1) + dot(
                local_sums[rows], neighbor_weight[...], 1, 1
            )

    outer_start(2)
    wb[...] = reduce_end(weigh, terms, "y", w1)
    weigh = reduce_start("x", wb, w2)
    outer_start(1)
    outer_pass(2)
    wc[...] = reduce_end(weigh, wb, "x", w2)
    weigh = reduce_start("z", wc, w3)
    outer_start(3)
    local_scatter(0)
    outer_pass(1)
    sums[at["y"], at["x"], at["z"]] = reduce_end(weigh, wc, "z", w3)
    weigh = give_start("z", gives["z"])
    outer_end(2)
    outer_start(0)
    local_scatter(1)
    outer_pass(3)
    outer_end(1)
    give_end(weigh, "z", gives["z"])
    weigh = give_start("x", gives["x"])
    outer_pass(0)
    local_scatter(2)
    outer_end(3)
    for chain in range(3):
        up, down = ways[chain][1]
        from_low, from_high, whole_low, whole_high = middle_recv[chain]
        n = middle_ids[chain]
        io.arrived(n[0], from_low, other)
        for k in range(2):
            add_into(firsts[chain].at[1, k], from_low.at[k])
        io.start(n[4], firsts[chain].at[1, low2], whole_low.at[low2], up)
        io.arrived(n[1], from_high, other)
        for k in range(2):
            add_into(firsts[chain].at[3, 2 + k], from_high.at[k])
        io.start(n[5], firsts[chain].at[3, high2], whole_high.at[high2], down)
    local_scatter(3)
    outer_end(0)
    give_end(weigh, "x", gives["x"])
    weigh = give_start("y", gives["y"])
    for chain in range(3):
        o, m, i = coords[chain]
        from_low, from_high, whole_low, whole_high = middle_recv[chain]
        n = middle_ids[chain]
        io.arrived(n[2], whole_low.at[high2], other)
        io.arrived(n[3], whole_high.at[low2], other)
        io.arrived(n[4], whole_low.at[low2], other)
        io.arrived(n[5], whole_high.at[high2], other)
        target = seconds[chain]
        for k in range(4):
            target[k] = three(firsts[chain].at[0, k], whole_low.at[k], whole_high.at[k]).astype(
                jnp.bfloat16
            )
        up, down = ways[chain][2]
        from_low, from_high, whole_low, whole_high = inner_recv[chain]
        n = inner_ids[chain]
        io.start(n[0], target.at[(i + 2) % 4, lowr], from_low, up)
        io.start(n[1], target.at[(i + 2) % 4, highr], from_high, down)
        io.start(n[2], target.at[(i + 1) % 4, highr], whole_low.at[highr], up)
        io.start(n[3], target.at[(i + 3) % 4, lowr], whole_high.at[lowr], down)
    for chain in range(3):
        o, m, i = coords[chain]
        up, down = ways[chain][2]
        target = seconds[chain]
        from_low, from_high, whole_low, whole_high = inner_recv[chain]
        n = inner_ids[chain]
        io.arrived(n[0], from_low, other)
        add_into(target.at[(i + 1) % 4, lowr], from_low)
        io.start(n[4], target.at[(i + 1) % 4, lowr], whole_low.at[lowr], up)
        io.arrived(n[1], from_high, other)
        add_into(target.at[(i + 3) % 4, highr], from_high)
        io.start(n[5], target.at[(i + 3) % 4, highr], whole_high.at[highr], down)
    products(0)
    products(1)
    last = [io.take() for _ in range(3)]
    for chain in range(3):
        o, m, i = coords[chain]
        from_low, from_high, whole_low, whole_high = inner_recv[chain]
        n = inner_ids[chain]
        io.arrived(n[2], whole_low.at[highr], other)
        io.arrived(n[3], whole_high.at[lowr], other)
        io.arrived(n[4], whole_low.at[lowr], other)
        io.arrived(n[5], whole_high.at[highr], other)
        results[chain][rep] = three(seconds[chain].at[i], whole_low, whole_high)
        io.start(last[chain], results[chain].at[rep], results[chain].at[rep], other)
    give_end(weigh, "y", gives["y"])
    for chain in range(3):
        io.arrived(last[chain], results[chain].at[1 - rep], other)
    output_done()
    tall = jnp.concatenate(
        [jnp.concatenate([r[0], r[1]], axis=1) for r in results], axis=0
    )
    value = dot((tall * (1.0 / 16.0)).astype(jnp.bfloat16), neighbor_weight[...], 1, 1)
    high = value.astype(jnp.bfloat16)
    low = (value - high.astype(jnp.float32)).astype(jnp.bfloat16)
    for begin in range(0, 2048, 512):
        rows = slice(begin, begin + 512)
        gradient[rows] = (
            total[rows, 0:128] + dot(chooser[rows], high) + dot(chooser[rows], low)
        ).astype(jnp.bfloat16)
    for n, target in enumerate((grad_self, grad_neighbor)):
        for h in range(2):
            for b in range(16):
                target[b * 8 : b * 8 + 8, h * 128 : h * 128 + 128] = (
                    sums[2 * n + h, b // 4, b % 4] * NORM
                )
    io.close()


def layer_call(features, cotangent, self_weight, neighbor_weight, raw, brows, hrows, lists, counts):
    args = (features, cotangent, self_weight, neighbor_weight, raw, brows, hrows, lists, counts)
    return pl.pallas_call(
        layer_kernel,
        out_shape=[jax.ShapeDtypeStruct((2048, 128), BF)] * 2
        + [jax.ShapeDtypeStruct((128, 256), F32)] * 2,
        in_specs=[VMEM_SPEC] * 8 + [pl.BlockSpec(memory_space=pltpu.SMEM)],
        out_specs=[VMEM_SPEC] * 4,
        scratch_shapes=[pltpu.VMEM(shape, kind) for _, shape, kind in SCRATCH]
        + [
            pltpu.SemaphoreType.DMA((N_COPIES,)),
            pltpu.SemaphoreType.DMA((N_COPIES,)),
            pltpu.SemaphoreType.DMA((4,)),
        ],
        compiler_params=pltpu.CompilerParams(
            collective_id=0, has_side_effects=True, vmem_limit_bytes=BIG
        ),
        name="layer",
    )(*args)


def per_device(
    features,
    cotangent,
    self_weight,
    neighbor_weight,
    local_neighbors,
    hub_rows,
    hub_neighbors,
    boundary_rows,
    send_lists,
    received_counts,
    halo_neighbors,
):
    raw = jnp.concatenate([local_neighbors.T, halo_neighbors.T, hub_neighbors.T], axis=0)
    output, gradient, grad_self, grad_neighbor = layer_call(
        features,
        cotangent,
        self_weight,
        neighbor_weight,
        raw,
        boundary_rows[None],
        hub_rows[None],
        send_lists.reshape(4, 4, 4, 1, 128),
        received_counts,
    )
    return output, gradient, grad_self, grad_neighbor


def solution(mesh):
    return jax.shard_map(
        per_device,
        mesh=mesh,
        in_specs=(
            P("dom", "rep"),
            P("dom", "rep"),
            P("rep", None),
            P("rep", None),
            P("dom", None),
            P("dom"),
            P("dom", None),
            P("dom"),
            P("dom", None, None),
            P("dom", None),
            P("dom", None),
        ),
        out_specs=(P("dom", "rep"), P("dom", "rep"), P("rep", None), P("rep", None)),
        check_vma=False,
    )
```

time: 970 us -> 118 us (0.12)
  the two profiles are of different devices: /device:TPU:0 before, /device:TPU:1 now
where the time goes in v2:
time: 118 us
  Pallas kernels  111 us (94%)
  local copies, waits for them, and re-layouts  4.56 us (4%)
  other arithmetic  1.55 us (1%)
    pallas_call x1, Pallas kernels, layer_call(): pl.pallas_call(layer_kernel, out_shape=[jax.ShapeDtypeStruct((2048, 128),...  111 us
    unnamed x10, local copies, waits for them, and re-layouts  4.56 us

profile of v2, /device:TPU:1, one launch (start us, length us, event | category | flops | bytes accessed | tf_op | source)
XLA Modules:
  0.0 117.9 jit_solution(6956650276710292233)
XLA Ops:
  0.6 1.6 %pad_add_fusion.refs_4_ = s32[16,2048]{1,0:T(8,128)} fusion(s32[4,2048]{1,0:T(4,128)} %bitcast.7, s32[4,2048]{1,0:T(4,128)} %bitcast.8, s32[8,2048]{1,0:T(8,128)} %bitcast.6), kind=kLoop, calls=%fused_computation | loop fusion | flops 65536 | bytes 262144 | tf_op jit(solution)/shard_map/concatenate | solution.py:908
  2.2 111.1 %layer.1 = (bf16[2048,128]{1,0:T(8,128)(2,1)}, bf16[2048,128]{1,0:T(8,128)(2,1)}, f32[128,256]{1,0:T(8,128)}, f32[128,256]{1,0:T(8,128)}) custom-call(bf16[2048,128]{1,0:T(8,128)(2,1)} %refs_0_.1, bf16[2048,128]{1,0:T(8,128)(2,1)} %refs_1_.1, bf16[128,256]{1,0:T(8,128)(2,1)} %refs_2_.1, bf16[128,256]{1,0:T(8,128)(2,1)} %refs_3_.1, ...), custom_call_target="tpu_custom_call" | custom-call | tf_op jit(solution)/shard_map/layer/pallas_call | solution.py:876
  113.3 0.0 copy-start
  113.3 1.9 %copy.19 = bf16[2048,128]{1,0:T(8,128)(2,1)} copy(bf16[2048,128]{1,0:T(8,128)(2,1)} %get-tuple-element.8) | data formatting | bytes 1048576
  115.2 0.0 copy-done
  115.2 0.0 copy-start.2
  115.2 0.8 copy.20
  116.0 0.2 copy-done.2
  116.2 0.0 copy-start.1
  116.2 0.7 copy.21
  116.9 0.3 copy-done.1
  117.2 0.7 copy.22
Async XLA Ops:
  113.3 1.9 %copy-start = (bf16[2048,128]{1,0:T(8,128)(2,1)S(1)}, bf16[2048,128]{1,0:T(8,128)(2,1)}, u32[]{:S(2)}) copy-start(bf16[2048,128]{1,0:T(8,128)(2,1)} %get-tuple-element.9) | copy-start | bytes 1572868
  115.2 1.0 copy-start.2
  116.2 1.0 copy-start.1

commit v3 on v2

--- a/solution.py
+++ b/solution.py
@@ -12,6 +12,8 @@
 STRIDE = {"y": 16, "x": 4, "z": 1}
 CHAINS = (("y", "x", "z"), ("z", "y", "x"), ("x", "z", "y"))
 UNIT = 96
+SHARE = (80, 128, 80)
+SHARE_AT = (0, 80, 208)
 BIG = 58 * 2**20
 
 
@@ -110,8 +112,8 @@
 SCRATCH = (
     [("g%d" % c, (4, 4, 4, UNIT, 128), BF) for c in range(3)]
     + [("x0", (4, 4, 2, UNIT, 128), BF), ("x1", (2, 4, 4, UNIT, 128), BF), ("x2", (4, 2, 4, UNIT, 128), BF)]
-    + [("give0", (4, 4, 2, UNIT, 128), BF), ("give1", (2, 4, 4, UNIT, 128), BF)]
-    + [("give2", (4, 2, 4, UNIT, 128), BF)]
+    + [("give0", (4, 4, 2, SHARE[0], 128), BF), ("give1", (2, 4, 4, SHARE[1], 128), BF)]
+    + [("give2", (4, 2, 4, SHARE[2], 128), BF)]
     + [(name, (4, 4, 4, 1, 128), I32) for name in ("l1", "l2", "l3")]
     + [("featx", (1024, 128), BF), ("cotx", (1024, 128), BF), ("wsx", (128, 256), BF), ("wnx", (128, 256), BF)]
     + [("chooser", (2048, 288), BF), ("units", (288, 128), BF)]
@@ -122,17 +124,14 @@
     + [("local_sums", (2048, 256), BF)]
     + [("w1", (3, 4, 4, 8, 128), F32), ("w2", (3, 4, 8, 128), F32), ("wb", (4, 4, 8, 128), F32)]
     + [("wc", (4, 8, 128), F32), ("w3", (3, 8, 128), F32)]
-    + [("r%d" % c, (2, UNIT, 128), F32) for c in range(3)]
-    + [("whole%d" % c, (4, 4, 4, UNIT, 128), BF) for c in range(3)]
-    + [("first%d" % c, (4, 4, UNIT, 128), BF) for c in range(3)]
-    + [("second%d" % c, (4, UNIT, 128), BF) for c in range(3)]
+    + [("r%d" % c, (2, SHARE[c], 128), F32) for c in range(3)]
+    + [("whole%d" % c, (4, 4, 4, SHARE[c], 128), BF) for c in range(3)]
+    + [("first%d" % c, (4, 4, SHARE[c], 128), BF) for c in range(3)]
+    + [("second%d" % c, (4, SHARE[c], 128), BF) for c in range(3)]
+    + [("inner%d" % c, (3, SHARE[c], 128), BF) for c in range(3)]
     + [
-        ("%s%d%d" % (stage, c, n), lead + ((shape[0] // 2,) + shape[1:] if n < 2 else shape), BF)
-        for stage, lead, shape in (
-            ("outer", (4,), (4, UNIT, 128)),
-            ("middle", (), (4, UNIT, 128)),
-            ("inner", (), (UNIT, 128)),
-        )
+        ("%s%d%d" % (stage, c, n), lead + (2 if n < 2 else 4, SHARE[c], 128), BF)
+        for stage, lead in (("outer", (4,)), ("middle", ()))
         for c in range(3)
         for n in range(4)
     ]
@@ -158,10 +157,11 @@
     wholes = [named["whole%d" % c] for c in range(3)]
     firsts = [named["first%d" % c] for c in range(3)]
     seconds = [named["second%d" % c] for c in range(3)]
-    outer_recv, middle_recv, inner_recv = (
+    outer_recv, middle_recv = (
         [[named["%s%d%d" % (stage, c, n)] for n in range(4)] for c in range(3)]
-        for stage in ("outer", "middle", "inner")
+        for stage in ("outer", "middle")
     )
+    inner_recv = [named["inner%d" % c] for c in range(3)]
     dom, rep, at = place()
     other = (dom, 1 - rep)
     io = Copies(send, recv)
@@ -220,14 +220,15 @@
         for chain in range(3)
     ]
 
-    inner_ids = [[io.take() for _ in range(4)] for _ in range(3)]
+    inner_ids = [[io.take() for _ in range(3)] for _ in range(3)]
     mine = []
     for chain in range(3):
         o, m, i = coords[chain]
-        up, down = ways[chain][2]
-        io.start(inner_ids[chain][0], units.at[pl.ds(chain * UNIT, UNIT)], bufs[chain].at[o, m, i], up)
-        io.start(inner_ids[chain][1], units.at[pl.ds(chain * UNIT, UNIT)], bufs[chain].at[o, m, i], down)
-        copy = pltpu.make_async_copy(units.at[pl.ds(chain * UNIT, UNIT)], bufs[chain].at[o, m, i], local.at[chain])
+        unit = units.at[pl.ds(chain * UNIT, UNIT)]
+        for delta in (1, 3, 2):
+            device = (shifted(dom, at, CHAINS[chain][2], delta), rep)
+            io.start(inner_ids[chain][delta - 1], unit, bufs[chain].at[o, m, i], device)
+        copy = pltpu.make_async_copy(unit, bufs[chain].at[o, m, i], local.at[chain])
         copy.start()
         mine.append(copy)
 
@@ -269,7 +270,6 @@
     for number, (src, dst) in zip(pair_ids, pairs):
         io.start(number, src, dst, other)
     listed = send_lists(0)
-    prepare()
 
     swap0, swap1, swap2 = io.used, io.used + 16, io.used + 24
     io.used += 32
@@ -320,36 +320,16 @@
         io.arrived(ids[1], from_up, up)
         io.start(ids[3], half(from_up, 1), half(from_up, 1), down)
 
-    def rows_half(ref, which):
-        return ref.at[pl.ds(which * (UNIT // 2), UNIT // 2)]
-
     def units_half(ref, which):
         return ref.at[pl.ds(which * 2, 2)]
 
-
-    def inner_pass():
-        for chain in range(3):
-            o, m, i = coords[chain]
-            up, down = ways[chain][2]
-            buf = bufs[chain]
-            pass_on(
-                chain,
-                inner_ids[chain],
-                buf.at[o, m, (i + 3) % 4],
-                buf.at[o, m, (i + 1) % 4],
-                rows_half,
-                up,
-                down,
-            )
 
     def inner_end():
         for chain in range(3):
             o, m, i = coords[chain]
-            up, down = ways[chain][2]
-            far = bufs[chain].at[o, m, (i + 2) % 4]
             mine[chain].wait()
-            io.arrived(inner_ids[chain][2], rows_half(far, 0), down)
-            io.arrived(inner_ids[chain][3], rows_half(far, 1), up)
+            for delta in (1, 3, 2):
+                io.arrived(inner_ids[chain][delta - 1], bufs[chain].at[o, m, (i - delta) % 4], other)
             up, down = ways[chain][1]
             block = bufs[chain].at[o, m]
             io.start(middle_ids[chain][0], block, block, up)
@@ -408,28 +388,28 @@
             io.arrived(outer_ids[chain][piece][3], units_half(far, 1), up)
             swap(chain, (o + 2) % 4, (m + piece) % 4)
 
-    inner_pass()
     inner_end()
+    prepare()
     take_lists(0, listed)
     listed = send_lists(1)
     for number, (_, dst) in zip(pair_ids, pairs):
         io.arrived(number, dst, other)
     own_rows = pl.ds(pl.multiple_of(rep * 1024, 1024), 1024)
     table[0:1024] = side_by_side(rep, features[own_rows], featx[...], 1)
-    local_gather(0)
     middle_pass()
     take_lists(1, listed)
     listed = send_lists(2)
     spread_pass(0)
-    local_gather(1)
     middle_end()
+    local_gather(0)
     spread_end(0)
     spread_pass(3)
+    local_gather(1)
+    spread_pass(1)
     local_gather(2)
-    spread_pass(1)
     spread_end(3)
+    spread_pass(2)
     local_gather(3)
-    spread_pass(2)
     take_lists(2, listed)
     spread_end(1)
     spread_end(2)
@@ -470,7 +450,7 @@
         table[pl.ds(pl.multiple_of(5120 + number * 32, 32), 32)] = wide[2][64:]
         return carry
 
-    lax.fori_loop(0, 32, select, 0)
+    lax.fori_loop(0, 32, select, 0, unroll=8)
 
     def gather_tile(tile):
         cols = pl.ds(pl.multiple_of(tile * 512, 512), 512)
@@ -574,9 +554,10 @@
             rows = jnp.concatenate([rows, hubs[k * 32 : k * 32 + 32]], axis=0)
             keep = jnp.where(rep == 0, rows[:, :128], rows[:, 128:])
             give = jnp.where(rep == 0, rows[:, 128:], rows[:, :128])
-            wholes[0][y, x, zz], give0[y, x, z] = keep[0:96], give[0:96]
-            wholes[1][zz, y, x], give1[z, y, x] = keep[96:192], give[96:192]
-            wholes[2][x, zz, y], give2[x, z, y] = keep[192:288], give[192:288]
+            parts = [slice(a, a + n) for a, n in zip(SHARE_AT, SHARE)]
+            wholes[0][y, x, zz], give0[y, x, z] = keep[parts[0]], give[parts[0]]
+            wholes[1][zz, y, x], give1[z, y, x] = keep[parts[1]], give[parts[1]]
+            wholes[2][x, zz, y], give2[x, z, y] = keep[parts[2]], give[parts[2]]
         return carry
 
     def output_done():
@@ -667,17 +648,10 @@
             got()
 
 
-    weigh = reduce_start("y", terms, w1)
-    lax.fori_loop(0, 8, scatter_step, 0)
-    for piece in ORDER:
-        for chain in range(3):
-            swap_start(chain, piece)
-
     outer_ids = [[[io.take() for _ in range(6)] for _ in range(4)] for _ in range(3)]
     middle_ids = [[io.take() for _ in range(6)] for _ in range(3)]
-    inner_ids = [[io.take() for _ in range(6)] for _ in range(3)]
+    inner_ids = [[io.take() for _ in range(3)] for _ in range(3)]
     low2, high2 = pl.ds(0, 2), pl.ds(2, 2)
-    lowr, highr = pl.ds(0, UNIT // 2), pl.ds(UNIT // 2, UNIT // 2)
 
     def add_into(spot, came):
         spot[...] = (spot[...].astype(jnp.float32) + came[...].astype(jnp.float32)).astype(jnp.bfloat16)
@@ -685,8 +659,8 @@
     def three(a, b, c):
         return a[...].astype(jnp.float32) + b[...].astype(jnp.float32) + c[...].astype(jnp.float32)
 
-    def outer_start(piece):
-        for chain in range(3):
+    def outer_start(piece, chains):
+        for chain in chains:
             swap_end(chain, piece)
             o, m, i = coords[chain]
             up, down = ways[chain][0]
@@ -698,8 +672,8 @@
             io.start(n[2], data.at[(o + 1) % 4, m, high2], whole_low.at[high2], up)
             io.start(n[3], data.at[(o + 3) % 4, m, low2], whole_high.at[low2], down)
 
-    def outer_pass(piece):
-        for chain in range(3):
+    def outer_pass(piece, chains):
+        for chain in chains:
             o, m, i = coords[chain]
             up, down = ways[chain][0]
             data, m = wholes[chain], (m + piece) % 4
@@ -714,8 +688,8 @@
                 add_into(data.at[(o + 3) % 4, m, 2 + k], from_high.at[k])
             io.start(n[5], data.at[(o + 3) % 4, m, high2], whole_high.at[high2], down)
 
-    def outer_end(piece):
-        for chain in range(3):
+    def outer_end(piece, chains):
+        for chain in chains:
             o, m, i = coords[chain]
             data, target = wholes[chain], firsts[chain].at[piece]
             _, _, whole_low, whole_high = (r.at[piece] for r in outer_recv[chain])
@@ -764,88 +738,116 @@
                 local_sums[rows], neighbor_weight[...], 1, 1
             )
 
-    outer_start(2)
+    def reduce_pass(chains):
+        for chain in chains:
+            up, down = ways[chain][1]
+            from_low, from_high, whole_low, whole_high = middle_recv[chain]
+            n = middle_ids[chain]
+            io.arrived(n[0], from_low, other)
+            for k in range(2):
+                add_into(firsts[chain].at[1, k], from_low.at[k])
+            io.start(n[4], firsts[chain].at[1, low2], whole_low.at[low2], up)
+            io.arrived(n[1], from_high, other)
+            for k in range(2):
+                add_into(firsts[chain].at[3, 2 + k], from_high.at[k])
+            io.start(n[5], firsts[chain].at[3, high2], whole_high.at[high2], down)
+
+    def reduce_last(chains):
+        for chain in chains:
+            o, m, i = coords[chain]
+            from_low, from_high, whole_low, whole_high = middle_recv[chain]
+            n = middle_ids[chain]
+            io.arrived(n[2], whole_low.at[high2], other)
+            io.arrived(n[3], whole_high.at[low2], other)
+            io.arrived(n[4], whole_low.at[low2], other)
+            io.arrived(n[5], whole_high.at[high2], other)
+            target = seconds[chain]
+            for k in range(4):
+                target[k] = three(
+                    firsts[chain].at[0, k], whole_low.at[k], whole_high.at[k]
+                ).astype(jnp.bfloat16)
+            for delta in (2, 1, 3):
+                device = (shifted(dom, at, CHAINS[chain][2], delta), rep)
+                io.start(
+                    inner_ids[chain][delta - 1],
+                    target.at[(i + delta) % 4],
+                    inner_recv[chain].at[delta - 1],
+                    device,
+                )
+
+    def scatter_piece(piece):
+        first = 2 * ((at["y"] + piece) % 4)
+        lax.fori_loop(0, 2, lambda k, carry: scatter_step(first + k, carry), 0)
+
+    early, late = (1,), (0, 2)
+    weigh = reduce_start("y", terms, w1)
+    scatter_piece(2)
+    swap_start(1, 2)
+    scatter_piece(1)
+    swap_start(1, 1)
+    outer_start(2, early)
     wb[...] = reduce_end(weigh, terms, "y", w1)
     weigh = reduce_start("x", wb, w2)
-    outer_start(1)
-    outer_pass(2)
+    scatter_piece(3)
+    swap_start(1, 3)
+    outer_start(1, early)
+    outer_pass(2, early)
     wc[...] = reduce_end(weigh, wb, "x", w2)
     weigh = reduce_start("z", wc, w3)
-    outer_start(3)
-    local_scatter(0)
-    outer_pass(1)
+    scatter_piece(0)
+    for piece in (2, 1):
+        for chain in late:
+            swap_start(chain, piece)
+    swap_start(1, 0)
+    for piece in (3, 0):
+        for chain in late:
+            swap_start(chain, piece)
+    outer_start(3, early)
+    outer_pass(1, early)
+    outer_end(2, early)
+    outer_start(2, late)
     sums[at["y"], at["x"], at["z"]] = reduce_end(weigh, wc, "z", w3)
     weigh = give_start("z", gives["z"])
-    outer_end(2)
-    outer_start(0)
+    outer_pass(3, early)
+    outer_start(1, late)
+    outer_end(1, early)
+    outer_pass(2, late)
+    outer_start(0, early)
+    outer_start(3, late)
+    outer_end(3, early)
+    local_scatter(0)
+    outer_pass(1, late)
+    outer_end(2, late)
+    outer_pass(0, early)
+    reduce_pass(early)
+    outer_start(0, late)
     local_scatter(1)
-    outer_pass(3)
-    outer_end(1)
+    outer_pass(3, late)
+    outer_end(1, late)
     give_end(weigh, "z", gives["z"])
     weigh = give_start("x", gives["x"])
-    outer_pass(0)
+    outer_end(0, early)
+    reduce_last(early)
+    outer_pass(0, late)
     local_scatter(2)
-    outer_end(3)
-    for chain in range(3):
-        up, down = ways[chain][1]
-        from_low, from_high, whole_low, whole_high = middle_recv[chain]
-        n = middle_ids[chain]
-        io.arrived(n[0], from_low, other)
-        for k in range(2):
-            add_into(firsts[chain].at[1, k], from_low.at[k])
-        io.start(n[4], firsts[chain].at[1, low2], whole_low.at[low2], up)
-        io.arrived(n[1], from_high, other)
-        for k in range(2):
-            add_into(firsts[chain].at[3, 2 + k], from_high.at[k])
-        io.start(n[5], firsts[chain].at[3, high2], whole_high.at[high2], down)
+    outer_end(3, late)
+    reduce_pass(late)
     local_scatter(3)
-    outer_end(0)
+    outer_end(0, late)
     give_end(weigh, "x", gives["x"])
     weigh = give_start("y", gives["y"])
-    for chain in range(3):
-        o, m, i = coords[chain]
-        from_low, from_high, whole_low, whole_high = middle_recv[chain]
-        n = middle_ids[chain]
-        io.arrived(n[2], whole_low.at[high2], other)
-        io.arrived(n[3], whole_high.at[low2], other)
-        io.arrived(n[4], whole_low.at[low2], other)
-        io.arrived(n[5], whole_high.at[high2], other)
-        target = seconds[chain]
-        for k in range(4):
-            target[k] = three(firsts[chain].at[0, k], whole_low.at[k], whole_high.at[k]).astype(
-                jnp.bfloat16
-            )
-        up, down = ways[chain][2]
-        from_low, from_high, whole_low, whole_high = inner_recv[chain]
-        n = inner_ids[chain]
-        io.start(n[0], target.at[(i + 2) % 4, lowr], from_low, up)
-        io.start(n[1], target.at[(i + 2) % 4, highr], from_high, down)
-        io.start(n[2], target.at[(i + 1) % 4, highr], whole_low.at[highr], up)
-        io.start(n[3], target.at[(i + 3) % 4, lowr], whole_high.at[lowr], down)
-    for chain in range(3):
-        o, m, i = coords[chain]
-        up, down = ways[chain][2]
-        target = seconds[chain]
-        from_low, from_high, whole_low, whole_high = inner_recv[chain]
-        n = inner_ids[chain]
-        io.arrived(n[0], from_low, other)
-        add_into(target.at[(i + 1) % 4, lowr], from_low)
-        io.start(n[4], target.at[(i + 1) % 4, lowr], whole_low.at[lowr], up)
-        io.arrived(n[1], from_high, other)
-        add_into(target.at[(i + 3) % 4, highr], from_high)
-        io.start(n[5], target.at[(i + 3) % 4, highr], whole_high.at[highr], down)
+    reduce_last(late)
     products(0)
     products(1)
     last = [io.take() for _ in range(3)]
-    for chain in range(3):
+    for chain in (1, 0, 2):
         o, m, i = coords[chain]
-        from_low, from_high, whole_low, whole_high = inner_recv[chain]
-        n = inner_ids[chain]
-        io.arrived(n[2], whole_low.at[highr], other)
-        io.arrived(n[3], whole_high.at[lowr], other)
-        io.arrived(n[4], whole_low.at[lowr], other)
-        io.arrived(n[5], whole_high.at[highr], other)
-        results[chain][rep] = three(seconds[chain].at[i], whole_low, whole_high)
+        came = inner_recv[chain]
+        for delta in (1, 3, 2):
+            io.arrived(inner_ids[chain][delta - 1], came.at[delta - 1], other)
+        results[chain][rep] = three(seconds[chain].at[i], came.at[0], came.at[2]) + came[1].astype(
+            jnp.float32
+        )
         io.start(last[chain], results[chain].at[rep], results[chain].at[rep], other)
     give_end(weigh, "y", gives["y"])
     for chain in range(3):
@@ -890,6 +892,21 @@
         ),
         name="layer",
     )(*args)
+
+
+def hand_over_kernel(*refs):
+    for source, target in zip(refs[:4], refs[4:]):
+        target[...] = source[...]
+
+
+def hand_over(*arrays):
+    return pl.pallas_call(
+        hand_over_kernel,
+        out_shape=[jax.ShapeDtypeStruct(a.shape, a.dtype) for a in arrays],
+        in_specs=[VMEM_SPEC] * 4,
+        out_specs=[VMEM_SPEC] * 4,
+        name="hand_over",
+    )(*arrays)
 
 
 def per_device(
@@ -917,7 +934,7 @@
         send_lists.reshape(4, 4, 4, 1, 128),
         received_counts,
     )
-    return output, gradient, grad_self, grad_neighbor
+    return tuple(hand_over(output, gradient, grad_self, grad_neighbor))
 
 
 def solution(mesh):

time: 118 us -> 105 us (0.89)
  Pallas kernels: 111 us -> 102 us
  local copies, waits for them, and re-layouts: 4.56 us -> 0 us
    pallas_call x1, Pallas kernels: 111 us -> 100 us  [layer_call(): pl.pallas_call(layer_kernel, out_shape=[jax.ShapeDtypeStruct((2048, 128),...]
    unnamed x10 -> x0, local copies, waits for them, and re-layouts: 4.56 us -> none
    pallas_call x0 -> x1, Pallas kernels: none -> 2.34 us  [hand_over(): pl.pallas_call(hand_over_kernel, out_shape=[jax.ShapeDtypeStruct(a.shape,...]
where the time goes in v3:
time: 105 us
  Pallas kernels  102 us (97%)
  other arithmetic  1.55 us (1%)
    pallas_call x1, Pallas kernels, layer_call(): pl.pallas_call(layer_kernel, out_shape=[jax.ShapeDtypeStruct((2048, 128),...  100 us
    pallas_call x1, Pallas kernels, hand_over(): pl.pallas_call(hand_over_kernel, out_shape=[jax.ShapeDtypeStruct(a.shape,...  2.34 us

profile of v3, /device:TPU:1, one launch (start us, length us, event | category | flops | bytes accessed | tf_op | source)
XLA Modules:
  0.0 104.6 jit_solution(7400425194993982174)
XLA Ops:
  0.6 1.6 %pad_add_fusion.refs_4_ = s32[16,2048]{1,0:T(8,128)} fusion(s32[4,2048]{1,0:T(4,128)} %bitcast.7, s32[4,2048]{1,0:T(4,128)} %bitcast.8, s32[8,2048]{1,0:T(8,128)} %bitcast.6), kind=kLoop, calls=%fused_computation | loop fusion | flops 65536 | bytes 262144 | tf_op jit(solution)/shard_map/concatenate | solution.py:925
  2.2 100.1 %layer.1 = (bf16[2048,128]{1,0:T(8,128)(2,1)}, bf16[2048,128]{1,0:T(8,128)(2,1)}, f32[128,256]{1,0:T(8,128)}, f32[128,256]{1,0:T(8,128)}) custom-call(bf16[2048,128]{1,0:T(8,128)(2,1)} %refs_0_.1, bf16[2048,128]{1,0:T(8,128)(2,1)} %refs_1_.1, bf16[128,256]{1,0:T(8,128)(2,1)} %refs_2_.1, bf16[128,256]{1,0:T(8,128)(2,1)} %refs_3_.1, ...), custom_call_target="tpu_custom_call" | custom-call | tf_op jit(solution)/shard_map/layer/pallas_call | solution.py:878
  102.3 2.3 %hand_over.1 = (bf16[2048,128]{1,0:T(8,128)(2,1)}, bf16[2048,128]{1,0:T(8,128)(2,1)}, f32[128,256]{1,0:T(8,128)}, f32[128,256]{1,0:T(8,128)}) custom-call(bf16[2048,128]{1,0:T(8,128)(2,1)} %get-tuple-element.8.refs_0_, bf16[2048,128]{1,0:T(8,128)(2,1)} %get-tuple-element.9.refs_1_, f32[128,256]{1,0:T(8,128)} %get-tuple-element.10.refs_2_, ...), custom_call_target="tpu_custom_call" | custom-call | tf_op jit(solution)/shard_map/hand_over/pallas_call | solution.py:903

commit v4 on v3

--- a/solution.py
+++ b/solution.py
@@ -139,10 +139,11 @@
 
 
 def layer_kernel(*refs):
-    (features, cotangent, self_weight, neighbor_weight, raw, brows, hrows, lists, counts) = refs[:9]
-    output, gradient, grad_self, grad_neighbor = refs[9:13]
-    named = {name: ref for (name, _, _), ref in zip(SCRATCH, refs[13:])}
-    send, recv, local = refs[13 + len(SCRATCH) :]
+    features, cotangent, self_weight, neighbor_weight, local_in, halo_in, hub_in = refs[:7]
+    brows, hrows, lists, counts = refs[7:11]
+    output, gradient, grad_self, grad_neighbor = refs[11:15]
+    named = {name: ref for (name, _, _), ref in zip(SCRATCH, refs[15:])}
+    send, recv, local = refs[15 + len(SCRATCH) :]
     g0, g1, g2 = bufs = [named["g%d" % c] for c in range(3)]
     x0, x1, x2 = [named["x%d" % c] for c in range(3)]
     give0, give1, give2 = [named["give%d" % c] for c in range(3)]
@@ -172,7 +173,7 @@
     pl.semaphore_wait(pltpu.get_barrier_semaphore(), 10)
 
     def prepare():
-        halo = raw[8:12]
+        halo = halo_in[...]
         end = jnp.int32(0)
         sender = jnp.zeros_like(halo)
         before = jnp.zeros_like(halo)
@@ -188,8 +189,8 @@
             number = (p >> 2) * 2 + (p & 1)
             return jnp.where(((p & 3) >> 1) == rep, number * size + within, -1)
 
-        hub = raw[12:16]
-        local = raw[0:8] - rep * 1024
+        hub = hub_in[...]
+        local = local_in[...] - rep * 1024
         local = jnp.where((local >= 0) & (local < 1024), local, -1)
         groups = (local, in_half(sender, slot, 128), in_half(hub >> 5, hub & 31, 32))
         start = 0
@@ -450,7 +451,7 @@
         table[pl.ds(pl.multiple_of(5120 + number * 32, 32), 32)] = wide[2][64:]
         return carry
 
-    lax.fori_loop(0, 32, select, 0, unroll=8)
+    lax.fori_loop(0, 32, select, 0, unroll=16)
 
     def gather_tile(tile):
         cols = pl.ds(pl.multiple_of(tile * 512, 512), 512)
@@ -528,11 +529,13 @@
         tall = pl.ds(pl.multiple_of((1 - rep) * 1024 + k * 512, 512), 512)
         io.arrived(grad_ids[k][0], grad.at[tall], other)
         io.arrived(grad_ids[k][1], agg_cols.at[tall], other)
-    for n, (mine_term, data) in enumerate(zip(own_terms, (features, agg_cols))):
-        term = mine_term + dot(data[theirs], grad[theirs], 0, 0)
-        for h in range(2):
-            for b in range(16):
-                terms[2 * n + h, b // 4, b % 4] = term[b * 8 : b * 8 + 8, h * 128 : h * 128 + 128]
+
+    def finish_terms():
+        for n, (mine_term, data) in enumerate(zip(own_terms, (features, agg_cols))):
+            term = mine_term + dot(data[theirs], grad[theirs], 0, 0)
+            for h in range(2):
+                for b in range(16):
+                    terms[2 * n + h, b // 4, b % 4] = term[b * 8 : b * 8 + 8, h * 128 : h * 128 + 128]
 
     def scatter_step(step, carry):
         sums_of = jnp.zeros((640, 256), jnp.float32)
@@ -780,20 +783,15 @@
         lax.fori_loop(0, 2, lambda k, carry: scatter_step(first + k, carry), 0)
 
     early, late = (1,), (0, 2)
-    weigh = reduce_start("y", terms, w1)
     scatter_piece(2)
     swap_start(1, 2)
     scatter_piece(1)
     swap_start(1, 1)
     outer_start(2, early)
-    wb[...] = reduce_end(weigh, terms, "y", w1)
-    weigh = reduce_start("x", wb, w2)
     scatter_piece(3)
     swap_start(1, 3)
     outer_start(1, early)
     outer_pass(2, early)
-    wc[...] = reduce_end(weigh, wb, "x", w2)
-    weigh = reduce_start("z", wc, w3)
     scatter_piece(0)
     for piece in (2, 1):
         for chain in late:
@@ -802,26 +800,33 @@
     for piece in (3, 0):
         for chain in late:
             swap_start(chain, piece)
+    finish_terms()
+    weigh = reduce_start("y", terms, w1)
     outer_start(3, early)
     outer_pass(1, early)
     outer_end(2, early)
     outer_start(2, late)
-    sums[at["y"], at["x"], at["z"]] = reduce_end(weigh, wc, "z", w3)
-    weigh = give_start("z", gives["z"])
+    local_scatter(0)
+    wb[...] = reduce_end(weigh, terms, "y", w1)
+    weigh = reduce_start("x", wb, w2)
     outer_pass(3, early)
     outer_start(1, late)
     outer_end(1, early)
     outer_pass(2, late)
     outer_start(0, early)
     outer_start(3, late)
+    wc[...] = reduce_end(weigh, wb, "x", w2)
+    weigh = reduce_start("z", wc, w3)
     outer_end(3, early)
-    local_scatter(0)
+    local_scatter(1)
     outer_pass(1, late)
     outer_end(2, late)
+    sums[at["y"], at["x"], at["z"]] = reduce_end(weigh, wc, "z", w3)
+    weigh = give_start("z", gives["z"])
     outer_pass(0, early)
     reduce_pass(early)
     outer_start(0, late)
-    local_scatter(1)
+    local_scatter(2)
     outer_pass(3, late)
     outer_end(1, late)
     give_end(weigh, "z", gives["z"])
@@ -829,14 +834,13 @@
     outer_end(0, early)
     reduce_last(early)
     outer_pass(0, late)
-    local_scatter(2)
+    local_scatter(3)
     outer_end(3, late)
     reduce_pass(late)
-    local_scatter(3)
     outer_end(0, late)
+    reduce_last(late)
     give_end(weigh, "x", gives["x"])
     weigh = give_start("y", gives["y"])
-    reduce_last(late)
     products(0)
     products(1)
     last = [io.take() for _ in range(3)]
@@ -859,10 +863,12 @@
     value = dot((tall * (1.0 / 16.0)).astype(jnp.bfloat16), neighbor_weight[...], 1, 1)
     high = value.astype(jnp.bfloat16)
     low = (value - high.astype(jnp.float32)).astype(jnp.bfloat16)
+    pieces = jnp.concatenate([high, low], axis=1)
     for begin in range(0, 2048, 512):
         rows = slice(begin, begin + 512)
+        both = dot(chooser[rows], pieces)
         gradient[rows] = (
-            total[rows, 0:128] + dot(chooser[rows], high) + dot(chooser[rows], low)
+            total[rows, 0:128] + both[:, 0:128] + both[:, 128:256]
         ).astype(jnp.bfloat16)
     for n, target in enumerate((grad_self, grad_neighbor)):
         for h in range(2):
@@ -873,13 +879,12 @@
     io.close()
 
 
-def layer_call(features, cotangent, self_weight, neighbor_weight, raw, brows, hrows, lists, counts):
-    args = (features, cotangent, self_weight, neighbor_weight, raw, brows, hrows, lists, counts)
+def layer_call(*args):
     return pl.pallas_call(
         layer_kernel,
         out_shape=[jax.ShapeDtypeStruct((2048, 128), BF)] * 2
         + [jax.ShapeDtypeStruct((128, 256), F32)] * 2,
-        in_specs=[VMEM_SPEC] * 8 + [pl.BlockSpec(memory_space=pltpu.SMEM)],
+        in_specs=[VMEM_SPEC] * 10 + [pl.BlockSpec(memory_space=pltpu.SMEM)],
         out_specs=[VMEM_SPEC] * 4,
         scratch_shapes=[pltpu.VMEM(shape, kind) for _, shape, kind in SCRATCH]
         + [
@@ -922,13 +927,14 @@
     received_counts,
     halo_neighbors,
 ):
-    raw = jnp.concatenate([local_neighbors.T, halo_neighbors.T, hub_neighbors.T], axis=0)
     output, gradient, grad_self, grad_neighbor = layer_call(
         features,
         cotangent,
         self_weight,
         neighbor_weight,
-        raw,
+        local_neighbors.T,
+        halo_neighbors.T,
+        hub_neighbors.T,
         boundary_rows[None],
         hub_rows[None],
         send_lists.reshape(4, 4, 4, 1, 128),

time: 105 us -> 102 us (0.971)
  other arithmetic: 1.55 us -> 0 us
    concatenate x1 -> x0, other arithmetic: 1.55 us -> none  [per_device(): jnp.concatenate([local_neighbors.T, halo_neighbors.T, hub_neighbors.T], a...]
    pallas_call x1, Pallas kernels: 100 us -> 98.8 us  [layer_call(): pl.pallas_call(layer_kernel, out_shape=[jax.ShapeDtypeStruct((2048, 128),...]
where the time goes in v4:
time: 102 us
  Pallas kernels  101 us (99%)
    pallas_call x1, Pallas kernels, layer_call(): pl.pallas_call(layer_kernel, out_shape=[jax.ShapeDtypeStruct((2048, 128),...  98.8 us
    pallas_call x1, Pallas kernels, hand_over(): pl.pallas_call(hand_over_kernel, out_shape=[jax.ShapeDtypeStruct(a.shape,...  2.34 us

profile of v4, /device:TPU:1, one launch (start us, length us, event | category | flops | bytes accessed | tf_op | source)
XLA Modules:
  0.0 101.8 jit_solution(4272461892611254854)
XLA Ops:
  0.6 98.8 %layer.1 = (bf16[2048,128]{1,0:T(8,128)(2,1)}, bf16[2048,128]{1,0:T(8,128)(2,1)}, f32[128,256]{1,0:T(8,128)}, f32[128,256]{1,0:T(8,128)}) custom-call(bf16[2048,128]{1,0:T(8,128)(2,1)} %refs_0_.1, bf16[2048,128]{1,0:T(8,128)(2,1)} %refs_1_.1, bf16[128,256]{1,0:T(8,128)(2,1)} %refs_2_.1, bf16[128,256]{1,0:T(8,128)(2,1)} %refs_3_.1, s32[8,2048]{1,0:T(8,128)} %bitcast.6, ...), custom_call_target="tpu_custom_call" | custom-call | tf_op jit(solution)/shard_map/layer/pallas_call | solution.py:883
  99.5 2.3 %hand_over.1 = (bf16[2048,128]{1,0:T(8,128)(2,1)}, bf16[2048,128]{1,0:T(8,128)(2,1)}, f32[128,256]{1,0:T(8,128)}, f32[128,256]{1,0:T(8,128)}) custom-call(bf16[2048,128]{1,0:T(8,128)(2,1)} %get-tuple-element.8.refs_0_, bf16[2048,128]{1,0:T(8,128)(2,1)} %get-tuple-element.9.refs_1_, f32[128,256]{1,0:T(8,128)} %get-tuple-element.10.refs_2_, ...), custom_call_target="tpu_custom_call" | custom-call | tf_op jit(solution)/shard_map/hand_over/pallas_call | solution.py:908

commit v5 on v4

--- a/solution.py
+++ b/solution.py
@@ -451,7 +451,7 @@
         table[pl.ds(pl.multiple_of(5120 + number * 32, 32), 32)] = wide[2][64:]
         return carry
 
-    lax.fori_loop(0, 32, select, 0, unroll=16)
+    lax.fori_loop(0, 32, select, 0, unroll=32)
 
     def gather_tile(tile):
         cols = pl.ds(pl.multiple_of(tile * 512, 512), 512)
@@ -854,6 +854,12 @@
         )
         io.start(last[chain], results[chain].at[rep], results[chain].at[rep], other)
     give_end(weigh, "y", gives["y"])
+    for n, target in enumerate((grad_self, grad_neighbor)):
+        for h in range(2):
+            for b in range(16):
+                target[b * 8 : b * 8 + 8, h * 128 : h * 128 + 128] = (
+                    sums[2 * n + h, b // 4, b % 4] * NORM
+                )
     for chain in range(3):
         io.arrived(last[chain], results[chain].at[1 - rep], other)
     output_done()
@@ -870,12 +876,6 @@
         gradient[rows] = (
             total[rows, 0:128] + both[:, 0:128] + both[:, 128:256]
         ).astype(jnp.bfloat16)
-    for n, target in enumerate((grad_self, grad_neighbor)):
-        for h in range(2):
-            for b in range(16):
-                target[b * 8 : b * 8 + 8, h * 128 : h * 128 + 128] = (
-                    sums[2 * n + h, b // 4, b % 4] * NORM
-                )
     io.close()
 
 

time: 102 us -> 102 us (level)
  no operation moved by 1% of the time
where the time goes in v5:
time: 102 us
  Pallas kernels  101 us (99%)
    pallas_call x1, Pallas kernels, layer_call(): pl.pallas_call(layer_kernel, out_shape=[jax.ShapeDtypeStruct((2048, 128),...  98.6 us
    pallas_call x1, Pallas kernels, hand_over(): pl.pallas_call(hand_over_kernel, out_shape=[jax.ShapeDtypeStruct(a.shape,...  2.34 us

profile of v5, /device:TPU:1, one launch (start us, length us, event | category | flops | bytes accessed | tf_op | source)
XLA Modules:
  0.0 101.5 jit_solution(17076814539811313333)
XLA Ops:
  0.6 98.6 %layer.1 = (bf16[2048,128]{1,0:T(8,128)(2,1)}, bf16[2048,128]{1,0:T(8,128)(2,1)}, f32[128,256]{1,0:T(8,128)}, f32[128,256]{1,0:T(8,128)}) custom-call(bf16[2048,128]{1,0:T(8,128)(2,1)} %refs_0_.1, bf16[2048,128]{1,0:T(8,128)(2,1)} %refs_1_.1, bf16[128,256]{1,0:T(8,128)(2,1)} %refs_2_.1, bf16[128,256]{1,0:T(8,128)(2,1)} %refs_3_.1, s32[8,2048]{1,0:T(8,128)} %bitcast.6, ...), custom_call_target="tpu_custom_call" | custom-call | tf_op jit(solution)/shard_map/layer/pallas_call | solution.py:883
  99.2 2.3 %hand_over.1 = (bf16[2048,128]{1,0:T(8,128)(2,1)}, bf16[2048,128]{1,0:T(8,128)(2,1)}, f32[128,256]{1,0:T(8,128)}, f32[128,256]{1,0:T(8,128)}) custom-call(bf16[2048,128]{1,0:T(8,128)(2,1)} %get-tuple-element.8.refs_0_, bf16[2048,128]{1,0:T(8,128)(2,1)} %get-tuple-element.9.refs_1_, f32[128,256]{1,0:T(8,128)} %get-tuple-element.10.refs_2_, ...), custom_call_target="tpu_custom_call" | custom-call | tf_op jit(solution)/shard_map/hand_over/pallas_call | solution.py:908
